TPU v7x, 32 devices: a whole 2x2x4 slice. The times are simulated.
32 devices in a mesh: group: 2 (over x), lev: 2 (over core), row: 8 (over z, y).
Axes of the slice: x: 2, y: 2, z: 4, core: 2. Of those that a mesh axis runs over, the one named last changes fastest.
Arguments:
- fields: bfloat16 [6, 90, 64, 1024], P('group', 'lev', 'row'), parts along dimension 0, may hold values from -6 to 6
- vertical_modes: bfloat16 [8, 90, 64, 1024], P(None, 'lev', 'row'), may hold values from -0.625 to 0.625
- diffusivity: float32 [64, 1024], P('row'), may hold values from 0.05 to 0.245
- land_mask: int32 [64, 1024], P('row'), may hold values 0 or 1
- wet_levels: int32 [64, 1024], P('row'), may hold values from 1 to 90
Outputs:
- filtered: bfloat16 [6, 90, 64, 1024], P('group', 'lev', 'row'), parts along dimension 0
- modal_flux: float32 [6, 8, 64, 1024], P('group', None, 'row', 'lev'), parts along dimension 0
There are 2 independent parts, one for each index of `group`. A program takes and returns all parts, laid end to end along the dimension named above; an argument that names none is the same for every part. Nothing has to cross between parts.
All inputs are finite; a program needn't handle non-finite values. No bound on the sum of `land_mask` on one device may be relied on, other than what follows from the above.
Results may differ from a plain program's by a relative error of at most 0.00092.
Values may be sent and summed in bfloat16 or wider, within the bound.
A program may use at most 192 MiB of HBM per device.

v0:
```python
import jax
import jax.numpy as jnp
from jax import lax
from jax.sharding import PartitionSpec as P

ITERS = 10


def extended_2(value, sides, width):
    for axis, dim in sides:
        size, length = (lax.axis_size(axis), value.shape[dim])
        up = [(i, (i + 1) % size) for i in range(size - 1)]
        down = [(j, i) for i, j in up]
        last = lax.slice_in_dim(value, length - width, length, axis=dim)
        first = lax.slice_in_dim(value, 0, width, axis=dim)
        before = lax.ppermute(last, axis, up)
        after = lax.ppermute(first, axis, down)
        value = jnp.concatenate([before, value, after], axis=dim)
    return value


def face_weights(diffusivity, wet_depth, lev_start, lev_count):
    level_index = lev_start + jnp.arange(lev_count, dtype=jnp.float32)
    wet_cells = (level_index[:, None, None] < wet_depth[None]).astype(jnp.float32)
    east_weight = (
        0.5
        * (diffusivity[:, :-1] + diffusivity[:, 1:])[None]
        * wet_cells[:, :, :-1]
        * wet_cells[:, :, 1:]
    )
    east_weight = jnp.pad(east_weight, ((0, 0), (0, 0), (0, 1)))
    north_weight = (
        0.5 * (diffusivity[:-1] + diffusivity[1:])[None] * wet_cells[:, :-1] * wet_cells[:, 1:]
    )
    north_weight = jnp.pad(north_weight, ((0, 0), (0, 1), (0, 0)))
    return (east_weight, north_weight)


def smooth(current, east_weight, north_weight):
    east_flux = east_weight * (jnp.roll(current, -1, 3) - current)
    north_flux = north_weight * (jnp.roll(current, -1, 2) - current)
    east_side = east_flux - jnp.roll(east_flux, 1, 3)
    north_side = north_flux - jnp.roll(north_flux, 1, 2)
    return current + east_side + north_side


def project(vertical_modes, rounded):
    return jnp.einsum(
        "klrc,flrc->fkrc", vertical_modes, rounded, preferred_element_type=jnp.float32
    )


def per_device(fields, vertical_modes, diffusivity, land_mask, wet_levels):
    lev_count = fields.shape[1]
    strip_rows = fields.shape[2]
    lev_start = (lax.axis_index("lev") * lev_count).astype(jnp.float32)
    wet_depth = (land_mask * wet_levels).astype(jnp.float32)
    statics = extended_2(jnp.stack([diffusivity, wet_depth]), (("row", 1),), 5)
    current = fields.astype(jnp.float32)
    east_weight, north_weight = face_weights(
        statics[0, 4 : strip_rows + 6], statics[1, 4 : strip_rows + 6], lev_start, lev_count
    )

    def one_step(step_index, present):
        extended = extended_2(present, (("row", 2),), 1)
        return smooth(extended, east_weight, north_weight)[:, :, 1 : strip_rows + 1]

    current = lax.fori_loop(0, ITERS, one_step, current)
    rounded = current.astype(jnp.bfloat16)
    amplitude = lax.psum_scatter(
        project(vertical_modes, rounded), "lev", scatter_dimension=3, tiled=True
    )
    modal_flux = jnp.stack(
        [
            amplitude[0] * amplitude[2],
            amplitude[1] * amplitude[2],
            0.5 * (amplitude[0] * amplitude[0] + amplitude[1] * amplitude[1]),
        ]
    )
    return (rounded, modal_flux)


def solution(mesh):
    placed = (
        P("group", "lev", "row", None),
        P(None, "lev", "row", None),
        P("row", None),
        P("row", None),
        P("row", None),
    )
    return jax.shard_map(
        per_device,
        mesh=mesh,
        in_specs=placed,
        out_specs=(P("group", "lev", "row", None), P("group", None, "row", "lev")),
        check_vma=False,
    )
```

profile of v0, /device:TPU:0, one launch (start us, length us, event | category | flops | bytes accessed | tf_op | source)
XLA Modules:
  0.0 884.3 jit_solution(4433715931043792953)
XLA Ops:
  19.3 13.3 %copy.23 = bf16[8,45,8,1024]{1,0,3,2:T(8,128)(2,1)} copy(bf16[8,45,8,1024]{3,2,1,0:T(8,128)(2,1)} %param.8) | data formatting | bytes 11796480 | tf_op args[1]
  38.9 760.0 %while.10 = (s32[]{:T(128)}, f32[3,45,8,1024]{3,2,1,0:T(8,128)}, f32[45,10,1024]{2,1,0:T(8,128)}, f32[45,10,1024]{2,1,0:T(8,128)}, s32[]{:T(128)}) while((s32[]{:T(128)}, f32[3,45,8,1024]{3,2,1,0:T(8,128)}, f32[45,10,1024]{2,1,0:T(8,128)}, f32[45,10,1024]{2,1,0:T(8,128)}, s32[]{:T(128)}) %tuple.35), condition=%wide.region_1.2_spmd, body=%wide.region_0.1_spmd.sunk | while | flops 21841920 | bytes 164055888 | solution.py:68
  60.2 12.0 %collective-permute-done.1 = f32[3,45,1,1024]{3,2,1,0:T(1,128)S(1)} collective-permute-done((f32[3,45,1,1024]{3,2,1,0:T(1,128)S(1)}, f32[3,45,1,1024]{3,2,1,0:T(1,128)S(1)}, u32[]{:S(2)}, u32[]{:S(2)}) %collective-permute-start.1) | collective-permute-done | bytes 552992 | tf_op jit(solution)/shard_map/while/body/eval_jaxpr/ppermute | solution.py:16
  97.2 17.1 %fusion.18 = f32[3,45,8,1024]{3,2,1,0:T(8,128)} fusion(f32[3,45,10,1024]{3,2,1,0:T(8,128)} %copy-done.2, f32[3,45,10,1024]{3,2,1,0:T(8,128)} %copy-done, f32[3,45,9,1024]{3,2,1,0:T(8,128)} %bitcast.20, f32[3,45,1,1024]{3,2,1,0:T(1,128)S(1)} %slice.173, f32[3,45,10,1024]{3,2,1,0:T(8,128)} %copy-done.1, f32[3,45,10,1023]{3,2,1,0:T(8,128)} %bitcast.19, ...), kind=kLoop, calls=%fused_computation.6.clone.1 | loop fusion | flops 6635520 | bytes 28753920 | tf_op jit(solution)/shard_map/while/body/eval_jaxpr/add | solution.py:44
  136.3 12.0 %collective-permute-done.1 = f32[3,45,1,1024]{3,2,1,0:T(1,128)S(1)} collective-permute-done((f32[3,45,1,1024]{3,2,1,0:T(1,128)S(1)}, f32[3,45,1,1024]{3,2,1,0:T(1,128)S(1)}, u32[]{:S(2)}, u32[]{:S(2)}) %collective-permute-start.1) | collective-permute-done | bytes 552992 | tf_op jit(solution)/shard_map/while/body/eval_jaxpr/ppermute | solution.py:16
  173.3 17.1 %fusion.18 = f32[3,45,8,1024]{3,2,1,0:T(8,128)} fusion(f32[3,45,10,1024]{3,2,1,0:T(8,128)} %copy-done.2, f32[3,45,10,1024]{3,2,1,0:T(8,128)} %copy-done, f32[3,45,9,1024]{3,2,1,0:T(8,128)} %bitcast.20, f32[3,45,1,1024]{3,2,1,0:T(1,128)S(1)} %slice.173, f32[3,45,10,1024]{3,2,1,0:T(8,128)} %copy-done.1, f32[3,45,10,1023]{3,2,1,0:T(8,128)} %bitcast.19, ...), kind=kLoop, calls=%fused_computation.6.clone.1 | loop fusion | flops 6635520 | bytes 28753920 | tf_op jit(solution)/shard_map/while/body/eval_jaxpr/add | solution.py:44
  201.6 10.8 %collective-permute-done = f32[3,45,1,1024]{3,2,1,0:T(1,128)S(1)} collective-permute-done((f32[3,45,1,1024]{3,2,1,0:T(1,128)S(1)}, f32[3,45,1,1024]{3,2,1,0:T(1,128)S(1)}, u32[]{:S(2)}, u32[]{:S(2)}) %collective-permute-start) | collective-permute-done | bytes 552992 | tf_op jit(solution)/shard_map/while/body/eval_jaxpr/ppermute | solution.py:17
  212.3 12.0 %collective-permute-done.1 = f32[3,45,1,1024]{3,2,1,0:T(1,128)S(1)} collective-permute-done((f32[3,45,1,1024]{3,2,1,0:T(1,128)S(1)}, f32[3,45,1,1024]{3,2,1,0:T(1,128)S(1)}, u32[]{:S(2)}, u32[]{:S(2)}) %collective-permute-start.1) | collective-permute-done | bytes 552992 | tf_op jit(solution)/shard_map/while/body/eval_jaxpr/ppermute | solution.py:16
  249.3 17.1 %fusion.18 = f32[3,45,8,1024]{3,2,1,0:T(8,128)} fusion(f32[3,45,10,1024]{3,2,1,0:T(8,128)} %copy-done.2, f32[3,45,10,1024]{3,2,1,0:T(8,128)} %copy-done, f32[3,45,9,1024]{3,2,1,0:T(8,128)} %bitcast.20, f32[3,45,1,1024]{3,2,1,0:T(1,128)S(1)} %slice.173, f32[3,45,10,1024]{3,2,1,0:T(8,128)} %copy-done.1, f32[3,45,10,1023]{3,2,1,0:T(8,128)} %bitcast.19, ...), kind=kLoop, calls=%fused_computation.6.clone.1 | loop fusion | flops 6635520 | bytes 28753920 | tf_op jit(solution)/shard_map/while/body/eval_jaxpr/add | solution.py:44
  277.6 10.8 %collective-permute-done = f32[3,45,1,1024]{3,2,1,0:T(1,128)S(1)} collective-permute-done((f32[3,45,1,1024]{3,2,1,0:T(1,128)S(1)}, f32[3,45,1,1024]{3,2,1,0:T(1,128)S(1)}, u32[]{:S(2)}, u32[]{:S(2)}) %collective-permute-start) | collective-permute-done | bytes 552992 | tf_op jit(solution)/shard_map/while/body/eval_jaxpr/ppermute | solution.py:17
  288.4 12.0 %collective-permute-done.1 = f32[3,45,1,1024]{3,2,1,0:T(1,128)S(1)} collective-permute-done((f32[3,45,1,1024]{3,2,1,0:T(1,128)S(1)}, f32[3,45,1,1024]{3,2,1,0:T(1,128)S(1)}, u32[]{:S(2)}, u32[]{:S(2)}) %collective-permute-start.1) | collective-permute-done | bytes 552992 | tf_op jit(solution)/shard_map/while/body/eval_jaxpr/ppermute | solution.py:16
  325.4 17.1 %fusion.18 = f32[3,45,8,1024]{3,2,1,0:T(8,128)} fusion(f32[3,45,10,1024]{3,2,1,0:T(8,128)} %copy-done.2, f32[3,45,10,1024]{3,2,1,0:T(8,128)} %copy-done, f32[3,45,9,1024]{3,2,1,0:T(8,128)} %bitcast.20, f32[3,45,1,1024]{3,2,1,0:T(1,128)S(1)} %slice.173, f32[3,45,10,1024]{3,2,1,0:T(8,128)} %copy-done.1, f32[3,45,10,1023]{3,2,1,0:T(8,128)} %bitcast.19, ...), kind=kLoop, calls=%fused_computation.6.clone.1 | loop fusion | flops 6635520 | bytes 28753920 | tf_op jit(solution)/shard_map/while/body/eval_jaxpr/add | solution.py:44
  353.7 10.8 %collective-permute-done = f32[3,45,1,1024]{3,2,1,0:T(1,128)S(1)} collective-permute-done((f32[3,45,1,1024]{3,2,1,0:T(1,128)S(1)}, f32[3,45,1,1024]{3,2,1,0:T(1,128)S(1)}, u32[]{:S(2)}, u32[]{:S(2)}) %collective-permute-start) | collective-permute-done | bytes 552992 | tf_op jit(solution)/shard_map/while/body/eval_jaxpr/ppermute | solution.py:17
  364.4 12.0 %collective-permute-done.1 = f32[3,45,1,1024]{3,2,1,0:T(1,128)S(1)} collective-permute-done((f32[3,45,1,1024]{3,2,1,0:T(1,128)S(1)}, f32[3,45,1,1024]{3,2,1,0:T(1,128)S(1)}, u32[]{:S(2)}, u32[]{:S(2)}) %collective-permute-start.1) | collective-permute-done | bytes 552992 | tf_op jit(solution)/shard_map/while/body/eval_jaxpr/ppermute | solution.py:16
  401.4 17.1 %fusion.18 = f32[3,45,8,1024]{3,2,1,0:T(8,128)} fusion(f32[3,45,10,1024]{3,2,1,0:T(8,128)} %copy-done.2, f32[3,45,10,1024]{3,2,1,0:T(8,128)} %copy-done, f32[3,45,9,1024]{3,2,1,0:T(8,128)} %bitcast.20, f32[3,45,1,1024]{3,2,1,0:T(1,128)S(1)} %slice.173, f32[3,45,10,1024]{3,2,1,0:T(8,128)} %copy-done.1, f32[3,45,10,1023]{3,2,1,0:T(8,128)} %bitcast.19, ...), kind=kLoop, calls=%fused_computation.6.clone.1 | loop fusion | flops 6635520 | bytes 28753920 | tf_op jit(solution)/shard_map/while/body/eval_jaxpr/add | solution.py:44
  429.7 10.8 %collective-permute-done = f32[3,45,1,1024]{3,2,1,0:T(1,128)S(1)} collective-permute-done((f32[3,45,1,1024]{3,2,1,0:T(1,128)S(1)}, f32[3,45,1,1024]{3,2,1,0:T(1,128)S(1)}, u32[]{:S(2)}, u32[]{:S(2)}) %collective-permute-start) | collective-permute-done | bytes 552992 | tf_op jit(solution)/shard_map/while/body/eval_jaxpr/ppermute | solution.py:17
  440.5 12.0 %collective-permute-done.1 = f32[3,45,1,1024]{3,2,1,0:T(1,128)S(1)} collective-permute-done((f32[3,45,1,1024]{3,2,1,0:T(1,128)S(1)}, f32[3,45,1,1024]{3,2,1,0:T(1,128)S(1)}, u32[]{:S(2)}, u32[]{:S(2)}) %collective-permute-start.1) | collective-permute-done | bytes 552992 | tf_op jit(solution)/shard_map/while/body/eval_jaxpr/ppermute | solution.py:16
  477.5 17.1 %fusion.18 = f32[3,45,8,1024]{3,2,1,0:T(8,128)} fusion(f32[3,45,10,1024]{3,2,1,0:T(8,128)} %copy-done.2, f32[3,45,10,1024]{3,2,1,0:T(8,128)} %copy-done, f32[3,45,9,1024]{3,2,1,0:T(8,128)} %bitcast.20, f32[3,45,1,1024]{3,2,1,0:T(1,128)S(1)} %slice.173, f32[3,45,10,1024]{3,2,1,0:T(8,128)} %copy-done.1, f32[3,45,10,1023]{3,2,1,0:T(8,128)} %bitcast.19, ...), kind=kLoop, calls=%fused_computation.6.clone.1 | loop fusion | flops 6635520 | bytes 28753920 | tf_op jit(solution)/shard_map/while/body/eval_jaxpr/add | solution.py:44
  505.8 10.8 %collective-permute-done = f32[3,45,1,1024]{3,2,1,0:T(1,128)S(1)} collective-permute-done((f32[3,45,1,1024]{3,2,1,0:T(1,128)S(1)}, f32[3,45,1,1024]{3,2,1,0:T(1,128)S(1)}, u32[]{:S(2)}, u32[]{:S(2)}) %collective-permute-start) | collective-permute-done | bytes 552992 | tf_op jit(solution)/shard_map/while/body/eval_jaxpr/ppermute | solution.py:17
  516.5 12.0 %collective-permute-done.1 = f32[3,45,1,1024]{3,2,1,0:T(1,128)S(1)} collective-permute-done((f32[3,45,1,1024]{3,2,1,0:T(1,128)S(1)}, f32[3,45,1,1024]{3,2,1,0:T(1,128)S(1)}, u32[]{:S(2)}, u32[]{:S(2)}) %collective-permute-start.1) | collective-permute-done | bytes 552992 | tf_op jit(solution)/shard_map/while/body/eval_jaxpr/ppermute | solution.py:16
  553.6 17.1 %fusion.18 = f32[3,45,8,1024]{3,2,1,0:T(8,128)} fusion(f32[3,45,10,1024]{3,2,1,0:T(8,128)} %copy-done.2, f32[3,45,10,1024]{3,2,1,0:T(8,128)} %copy-done, f32[3,45,9,1024]{3,2,1,0:T(8,128)} %bitcast.20, f32[3,45,1,1024]{3,2,1,0:T(1,128)S(1)} %slice.173, f32[3,45,10,1024]{3,2,1,0:T(8,128)} %copy-done.1, f32[3,45,10,1023]{3,2,1,0:T(8,128)} %bitcast.19, ...), kind=kLoop, calls=%fused_computation.6.clone.1 | loop fusion | flops 6635520 | bytes 28753920 | tf_op jit(solution)/shard_map/while/body/eval_jaxpr/add | solution.py:44
  581.9 10.8 %collective-permute-done = f32[3,45,1,1024]{3,2,1,0:T(1,128)S(1)} collective-permute-done((f32[3,45,1,1024]{3,2,1,0:T(1,128)S(1)}, f32[3,45,1,1024]{3,2,1,0:T(1,128)S(1)}, u32[]{:S(2)}, u32[]{:S(2)}) %collective-permute-start) | collective-permute-done | bytes 552992 | tf_op jit(solution)/shard_map/while/body/eval_jaxpr/ppermute | solution.py:17
  592.6 12.0 %collective-permute-done.1 = f32[3,45,1,1024]{3,2,1,0:T(1,128)S(1)} collective-permute-done((f32[3,45,1,1024]{3,2,1,0:T(1,128)S(1)}, f32[3,45,1,1024]{3,2,1,0:T(1,128)S(1)}, u32[]{:S(2)}, u32[]{:S(2)}) %collective-permute-start.1) | collective-permute-done | bytes 552992 | tf_op jit(solution)/shard_map/while/body/eval_jaxpr/ppermute | solution.py:16
  629.6 17.1 %fusion.18 = f32[3,45,8,1024]{3,2,1,0:T(8,128)} fusion(f32[3,45,10,1024]{3,2,1,0:T(8,128)} %copy-done.2, f32[3,45,10,1024]{3,2,1,0:T(8,128)} %copy-done, f32[3,45,9,1024]{3,2,1,0:T(8,128)} %bitcast.20, f32[3,45,1,1024]{3,2,1,0:T(1,128)S(1)} %slice.173, f32[3,45,10,1024]{3,2,1,0:T(8,128)} %copy-done.1, f32[3,45,10,1023]{3,2,1,0:T(8,128)} %bitcast.19, ...), kind=kLoop, calls=%fused_computation.6.clone.1 | loop fusion | flops 6635520 | bytes 28753920 | tf_op jit(solution)/shard_map/while/body/eval_jaxpr/add | solution.py:44
  657.9 10.8 %collective-permute-done = f32[3,45,1,1024]{3,2,1,0:T(1,128)S(1)} collective-permute-done((f32[3,45,1,1024]{3,2,1,0:T(1,128)S(1)}, f32[3,45,1,1024]{3,2,1,0:T(1,128)S(1)}, u32[]{:S(2)}, u32[]{:S(2)}) %collective-permute-start) | collective-permute-done | bytes 552992 | tf_op jit(solution)/shard_map/while/body/eval_jaxpr/ppermute | solution.py:17
  668.7 12.0 %collective-permute-done.1 = f32[3,45,1,1024]{3,2,1,0:T(1,128)S(1)} collective-permute-done((f32[3,45,1,1024]{3,2,1,0:T(1,128)S(1)}, f32[3,45,1,1024]{3,2,1,0:T(1,128)S(1)}, u32[]{:S(2)}, u32[]{:S(2)}) %collective-permute-start.1) | collective-permute-done | bytes 552992 | tf_op jit(solution)/shard_map/while/body/eval_jaxpr/ppermute | solution.py:16
  705.7 17.1 %fusion.18 = f32[3,45,8,1024]{3,2,1,0:T(8,128)} fusion(f32[3,45,10,1024]{3,2,1,0:T(8,128)} %copy-done.2, f32[3,45,10,1024]{3,2,1,0:T(8,128)} %copy-done, f32[3,45,9,1024]{3,2,1,0:T(8,128)} %bitcast.20, f32[3,45,1,1024]{3,2,1,0:T(1,128)S(1)} %slice.173, f32[3,45,10,1024]{3,2,1,0:T(8,128)} %copy-done.1, f32[3,45,10,1023]{3,2,1,0:T(8,128)} %bitcast.19, ...), kind=kLoop, calls=%fused_computation.6.clone.1 | loop fusion | flops 6635520 | bytes 28753920 | tf_op jit(solution)/shard_map/while/body/eval_jaxpr/add | solution.py:44
  744.7 12.0 %collective-permute-done.1 = f32[3,45,1,1024]{3,2,1,0:T(1,128)S(1)} collective-permute-done((f32[3,45,1,1024]{3,2,1,0:T(1,128)S(1)}, f32[3,45,1,1024]{3,2,1,0:T(1,128)S(1)}, u32[]{:S(2)}, u32[]{:S(2)}) %collective-permute-start.1) | collective-permute-done | bytes 552992 | tf_op jit(solution)/shard_map/while/body/eval_jaxpr/ppermute | solution.py:16
  781.7 17.1 %fusion.18 = f32[3,45,8,1024]{3,2,1,0:T(8,128)} fusion(f32[3,45,10,1024]{3,2,1,0:T(8,128)} %copy-done.2, f32[3,45,10,1024]{3,2,1,0:T(8,128)} %copy-done, f32[3,45,9,1024]{3,2,1,0:T(8,128)} %bitcast.20, f32[3,45,1,1024]{3,2,1,0:T(1,128)S(1)} %slice.173, f32[3,45,10,1024]{3,2,1,0:T(8,128)} %copy-done.1, f32[3,45,10,1023]{3,2,1,0:T(8,128)} %bitcast.19, ...), kind=kLoop, calls=%fused_computation.6.clone.1 | loop fusion | flops 6635520 | bytes 28753920 | tf_op jit(solution)/shard_map/while/body/eval_jaxpr/add | solution.py:44
  808.3 17.6 %convolution_bitcast_fusion = f32[3,8,8,1024]{1,0,3,2:T(4,128)} fusion(bf16[3,45,8,1024]{1,0,3,2:T(4,128)(2,1)} %copy.22, bf16[8,45,8,1024]{1,0,3,2:T(8,128)(2,1)} %copy.23), kind=kOutput, calls=%fused_computation.11 | convolution fusion | flops 17694720 | bytes 8896512 | tf_op jit(solution)/shard_map/klrc,flrc->fkrc/dot_general | solution.py:48
  825.9 17.6 %copy.24 = f32[3,8,8,1024]{2,1,0,3:T(8,128)} copy(f32[3,8,8,1024]{1,0,3,2:T(4,128)} %convolution_bitcast_fusion) | data formatting | bytes 1572864 | tf_op jit(solution)/shard_map/klrc,flrc->fkrc/transpose | solution.py:48
  843.5 22.8 %reduce-scatter.2.cloned.1.call-done = f32[3,8,8,512]{2,1,0,3:T(8,128)} async-done(((f32[3,8,8,1024]{2,1,0,3:T(8,128)}), f32[3,8,8,512]{2,1,0,3:T(8,128)}) %reduce-scatter.2.cloned.1.call-update) | async-done | bytes 393232 | tf_op jit(solution)/shard_map/reduce_scatter | solution.py:70
  (233 shorter events, 431.4 us)
Async XLA Ops:
  7.2 859.2 %reduce-scatter.2.cloned.1.call-start = ((), (), s32[]{:S(2)}) async-start(), calls=%async_computation.1 | async-start | bytes 18874368 | tf_op jit(solution)/shard_map/reduce_scatter | solution.py:70
  8.8 23.8 %collective-permute-start.2 = (f32[2,5,1024]{2,1,0:T(8,128)S(1)}, f32[2,5,1024]{2,1,0:T(8,128)S(1)}, u32[]{:S(2)}, u32[]{:S(2)}) collective-permute-start(f32[2,5,1024]{2,1,0:T(8,128)S(1)} %get-tuple-element.47), channel_id=1, source_target_pairs={{0,1},{1,2},{2,3},{3,4},{4,5},{5,6},{6,7},{8,9},{9,10},{10,11},{11... | collective-permute-start | bytes 122888 | tf_op jit(solution)/shard_map/ppermute | solution.py:16
  13.7 18.9 %collective-permute-start.3 = (f32[2,5,1024]{2,1,0:T(8,128)S(1)}, f32[2,5,1024]{2,1,0:T(8,128)S(1)}, u32[]{:S(2)}, u32[]{:S(2)}) collective-permute-start(f32[2,5,1024]{2,1,0:T(8,128)S(1)} %get-tuple-element.48), channel_id=1, source_target_pairs={{1,0},{2,1},{3,2},{4,3},{5,4},{6,5},{7,6},{9,8},{10,9},{11,10},{12... | collective-permute-start | bytes 122888 | tf_op jit(solution)/shard_map/ppermute | solution.py:17
  19.3 13.3 %copy-start.4 = (f32[8,1024]{1,0:T(8,128)S(1)}, f32[8,1024]{1,0:T(8,128)}, u32[]{:S(2)}) copy-start(f32[8,1024]{1,0:T(8,128)} %param.9) | copy-start | bytes 98308
  43.7 16.5 %collective-permute-start = (f32[3,45,1,1024]{3,2,1,0:T(1,128)S(1)}, f32[3,45,1,1024]{3,2,1,0:T(1,128)S(1)}, u32[]{:S(2)}, u32[]{:S(2)}) collective-permute-start(f32[3,45,1,1024]{3,2,1,0:T(1,128)S(1)} %get-tuple-element.78), channel_id=1, source_target_pairs={{1,0},{2,1},{3,2},{4,3},{5,4},{6,5},{7,6},{9,8},{10,9},{11,10},{12... | collective-permute-start | bytes 1658888 | tf_op jit(solution)/shard_map/while/body/eval_jaxpr/ppermute | solution.py:17
  45.0 27.2 %collective-permute-start.1 = (f32[3,45,1,1024]{3,2,1,0:T(1,128)S(1)}, f32[3,45,1,1024]{3,2,1,0:T(1,128)S(1)}, u32[]{:S(2)}, u32[]{:S(2)}) collective-permute-start(f32[3,45,1,1024]{3,2,1,0:T(1,128)S(1)} %get-tuple-element.79), channel_id=1, source_target_pairs={{0,1},{1,2},{2,3},{3,4},{4,5},{5,6},{6,7},{8,9},{9,10},{10,11},{11... | collective-permute-start | bytes 1658888 | tf_op jit(solution)/shard_map/while/body/eval_jaxpr/ppermute | solution.py:16
  75.7 7.2 copy-start
  119.2 17.1 %collective-permute-start = (f32[3,45,1,1024]{3,2,1,0:T(1,128)S(1)}, f32[3,45,1,1024]{3,2,1,0:T(1,128)S(1)}, u32[]{:S(2)}, u32[]{:S(2)}) collective-permute-start(f32[3,45,1,1024]{3,2,1,0:T(1,128)S(1)} %get-tuple-element.78), channel_id=1, source_target_pairs={{1,0},{2,1},{3,2},{4,3},{5,4},{6,5},{7,6},{9,8},{10,9},{11,10},{12... | collective-permute-start | bytes 1658888 | tf_op jit(solution)/shard_map/while/body/eval_jaxpr/ppermute | solution.py:17
  120.5 27.8 %collective-permute-start.1 = (f32[3,45,1,1024]{3,2,1,0:T(1,128)S(1)}, f32[3,45,1,1024]{3,2,1,0:T(1,128)S(1)}, u32[]{:S(2)}, u32[]{:S(2)}) collective-permute-start(f32[3,45,1,1024]{3,2,1,0:T(1,128)S(1)} %get-tuple-element.79), channel_id=1, source_target_pairs={{0,1},{1,2},{2,3},{3,4},{4,5},{5,6},{6,7},{8,9},{9,10},{10,11},{11... | collective-permute-start | bytes 1658888 | tf_op jit(solution)/shard_map/while/body/eval_jaxpr/ppermute | solution.py:16
  151.7 7.2 copy-start
  195.2 17.1 %collective-permute-start = (f32[3,45,1,1024]{3,2,1,0:T(1,128)S(1)}, f32[3,45,1,1024]{3,2,1,0:T(1,128)S(1)}, u32[]{:S(2)}, u32[]{:S(2)}) collective-permute-start(f32[3,45,1,1024]{3,2,1,0:T(1,128)S(1)} %get-tuple-element.78), channel_id=1, source_target_pairs={{1,0},{2,1},{3,2},{4,3},{5,4},{6,5},{7,6},{9,8},{10,9},{11,10},{12... | collective-permute-start | bytes 1658888 | tf_op jit(solution)/shard_map/while/body/eval_jaxpr/ppermute | solution.py:17
  196.5 27.8 %collective-permute-start.1 = (f32[3,45,1,1024]{3,2,1,0:T(1,128)S(1)}, f32[3,45,1,1024]{3,2,1,0:T(1,128)S(1)}, u32[]{:S(2)}, u32[]{:S(2)}) collective-permute-start(f32[3,45,1,1024]{3,2,1,0:T(1,128)S(1)} %get-tuple-element.79), channel_id=1, source_target_pairs={{0,1},{1,2},{2,3},{3,4},{4,5},{5,6},{6,7},{8,9},{9,10},{10,11},{11... | collective-permute-start | bytes 1658888 | tf_op jit(solution)/shard_map/while/body/eval_jaxpr/ppermute | solution.py:16
  227.8 7.2 copy-start
  271.3 17.1 %collective-permute-start = (f32[3,45,1,1024]{3,2,1,0:T(1,128)S(1)}, f32[3,45,1,1024]{3,2,1,0:T(1,128)S(1)}, u32[]{:S(2)}, u32[]{:S(2)}) collective-permute-start(f32[3,45,1,1024]{3,2,1,0:T(1,128)S(1)} %get-tuple-element.78), channel_id=1, source_target_pairs={{1,0},{2,1},{3,2},{4,3},{5,4},{6,5},{7,6},{9,8},{10,9},{11,10},{12... | collective-permute-start | bytes 1658888 | tf_op jit(solution)/shard_map/while/body/eval_jaxpr/ppermute | solution.py:17
  272.6 27.8 %collective-permute-start.1 = (f32[3,45,1,1024]{3,2,1,0:T(1,128)S(1)}, f32[3,45,1,1024]{3,2,1,0:T(1,128)S(1)}, u32[]{:S(2)}, u32[]{:S(2)}) collective-permute-start(f32[3,45,1,1024]{3,2,1,0:T(1,128)S(1)} %get-tuple-element.79), channel_id=1, source_target_pairs={{0,1},{1,2},{2,3},{3,4},{4,5},{5,6},{6,7},{8,9},{9,10},{10,11},{11... | collective-permute-start | bytes 1658888 | tf_op jit(solution)/shard_map/while/body/eval_jaxpr/ppermute | solution.py:16
  303.8 7.2 copy-start
  347.3 17.1 %collective-permute-start = (f32[3,45,1,1024]{3,2,1,0:T(1,128)S(1)}, f32[3,45,1,1024]{3,2,1,0:T(1,128)S(1)}, u32[]{:S(2)}, u32[]{:S(2)}) collective-permute-start(f32[3,45,1,1024]{3,2,1,0:T(1,128)S(1)} %get-tuple-element.78), channel_id=1, source_target_pairs={{1,0},{2,1},{3,2},{4,3},{5,4},{6,5},{7,6},{9,8},{10,9},{11,10},{12... | collective-permute-start | bytes 1658888 | tf_op jit(solution)/shard_map/while/body/eval_jaxpr/ppermute | solution.py:17
  348.6 27.8 %collective-permute-start.1 = (f32[3,45,1,1024]{3,2,1,0:T(1,128)S(1)}, f32[3,45,1,1024]{3,2,1,0:T(1,128)S(1)}, u32[]{:S(2)}, u32[]{:S(2)}) collective-permute-start(f32[3,45,1,1024]{3,2,1,0:T(1,128)S(1)} %get-tuple-element.79), channel_id=1, source_target_pairs={{0,1},{1,2},{2,3},{3,4},{4,5},{5,6},{6,7},{8,9},{9,10},{10,11},{11... | collective-permute-start | bytes 1658888 | tf_op jit(solution)/shard_map/while/body/eval_jaxpr/ppermute | solution.py:16
  379.9 7.2 copy-start
  423.4 17.1 %collective-permute-start = (f32[3,45,1,1024]{3,2,1,0:T(1,128)S(1)}, f32[3,45,1,1024]{3,2,1,0:T(1,128)S(1)}, u32[]{:S(2)}, u32[]{:S(2)}) collective-permute-start(f32[3,45,1,1024]{3,2,1,0:T(1,128)S(1)} %get-tuple-element.78), channel_id=1, source_target_pairs={{1,0},{2,1},{3,2},{4,3},{5,4},{6,5},{7,6},{9,8},{10,9},{11,10},{12... | collective-permute-start | bytes 1658888 | tf_op jit(solution)/shard_map/while/body/eval_jaxpr/ppermute | solution.py:17
  424.7 27.8 %collective-permute-start.1 = (f32[3,45,1,1024]{3,2,1,0:T(1,128)S(1)}, f32[3,45,1,1024]{3,2,1,0:T(1,128)S(1)}, u32[]{:S(2)}, u32[]{:S(2)}) collective-permute-start(f32[3,45,1,1024]{3,2,1,0:T(1,128)S(1)} %get-tuple-element.79), channel_id=1, source_target_pairs={{0,1},{1,2},{2,3},{3,4},{4,5},{5,6},{6,7},{8,9},{9,10},{10,11},{11... | collective-permute-start | bytes 1658888 | tf_op jit(solution)/shard_map/while/body/eval_jaxpr/ppermute | solution.py:16
  455.9 7.2 copy-start
  499.4 17.1 %collective-permute-start = (f32[3,45,1,1024]{3,2,1,0:T(1,128)S(1)}, f32[3,45,1,1024]{3,2,1,0:T(1,128)S(1)}, u32[]{:S(2)}, u32[]{:S(2)}) collective-permute-start(f32[3,45,1,1024]{3,2,1,0:T(1,128)S(1)} %get-tuple-element.78), channel_id=1, source_target_pairs={{1,0},{2,1},{3,2},{4,3},{5,4},{6,5},{7,6},{9,8},{10,9},{11,10},{12... | collective-permute-start | bytes 1658888 | tf_op jit(solution)/shard_map/while/body/eval_jaxpr/ppermute | solution.py:17
  500.7 27.8 %collective-permute-start.1 = (f32[3,45,1,1024]{3,2,1,0:T(1,128)S(1)}, f32[3,45,1,1024]{3,2,1,0:T(1,128)S(1)}, u32[]{:S(2)}, u32[]{:S(2)}) collective-permute-start(f32[3,45,1,1024]{3,2,1,0:T(1,128)S(1)} %get-tuple-element.79), channel_id=1, source_target_pairs={{0,1},{1,2},{2,3},{3,4},{4,5},{5,6},{6,7},{8,9},{9,10},{10,11},{11... | collective-permute-start | bytes 1658888 | tf_op jit(solution)/shard_map/while/body/eval_jaxpr/ppermute | solution.py:16
  532.0 7.2 copy-start
  575.5 17.1 %collective-permute-start = (f32[3,45,1,1024]{3,2,1,0:T(1,128)S(1)}, f32[3,45,1,1024]{3,2,1,0:T(1,128)S(1)}, u32[]{:S(2)}, u32[]{:S(2)}) collective-permute-start(f32[3,45,1,1024]{3,2,1,0:T(1,128)S(1)} %get-tuple-element.78), channel_id=1, source_target_pairs={{1,0},{2,1},{3,2},{4,3},{5,4},{6,5},{7,6},{9,8},{10,9},{11,10},{12... | collective-permute-start | bytes 1658888 | tf_op jit(solution)/shard_map/while/body/eval_jaxpr/ppermute | solution.py:17
  576.8 27.8 %collective-permute-start.1 = (f32[3,45,1,1024]{3,2,1,0:T(1,128)S(1)}, f32[3,45,1,1024]{3,2,1,0:T(1,128)S(1)}, u32[]{:S(2)}, u32[]{:S(2)}) collective-permute-start(f32[3,45,1,1024]{3,2,1,0:T(1,128)S(1)} %get-tuple-element.79), channel_id=1, source_target_pairs={{0,1},{1,2},{2,3},{3,4},{4,5},{5,6},{6,7},{8,9},{9,10},{10,11},{11... | collective-permute-start | bytes 1658888 | tf_op jit(solution)/shard_map/while/body/eval_jaxpr/ppermute | solution.py:16
  651.6 17.1 %collective-permute-start = (f32[3,45,1,1024]{3,2,1,0:T(1,128)S(1)}, f32[3,45,1,1024]{3,2,1,0:T(1,128)S(1)}, u32[]{:S(2)}, u32[]{:S(2)}) collective-permute-start(f32[3,45,1,1024]{3,2,1,0:T(1,128)S(1)} %get-tuple-element.78), channel_id=1, source_target_pairs={{1,0},{2,1},{3,2},{4,3},{5,4},{6,5},{7,6},{9,8},{10,9},{11,10},{12... | collective-permute-start | bytes 1658888 | tf_op jit(solution)/shard_map/while/body/eval_jaxpr/ppermute | solution.py:17
  652.9 27.8 %collective-permute-start.1 = (f32[3,45,1,1024]{3,2,1,0:T(1,128)S(1)}, f32[3,45,1,1024]{3,2,1,0:T(1,128)S(1)}, u32[]{:S(2)}, u32[]{:S(2)}) collective-permute-start(f32[3,45,1,1024]{3,2,1,0:T(1,128)S(1)} %get-tuple-element.79), channel_id=1, source_target_pairs={{0,1},{1,2},{2,3},{3,4},{4,5},{5,6},{6,7},{8,9},{9,10},{10,11},{11... | collective-permute-start | bytes 1658888 | tf_op jit(solution)/shard_map/while/body/eval_jaxpr/ppermute | solution.py:16
  684.1 7.2 copy-start
  727.6 17.1 %collective-permute-start = (f32[3,45,1,1024]{3,2,1,0:T(1,128)S(1)}, f32[3,45,1,1024]{3,2,1,0:T(1,128)S(1)}, u32[]{:S(2)}, u32[]{:S(2)}) collective-permute-start(f32[3,45,1,1024]{3,2,1,0:T(1,128)S(1)} %get-tuple-element.78), channel_id=1, source_target_pairs={{1,0},{2,1},{3,2},{4,3},{5,4},{6,5},{7,6},{9,8},{10,9},{11,10},{12... | collective-permute-start | bytes 1658888 | tf_op jit(solution)/shard_map/while/body/eval_jaxpr/ppermute | solution.py:17
  728.9 27.8 %collective-permute-start.1 = (f32[3,45,1,1024]{3,2,1,0:T(1,128)S(1)}, f32[3,45,1,1024]{3,2,1,0:T(1,128)S(1)}, u32[]{:S(2)}, u32[]{:S(2)}) collective-permute-start(f32[3,45,1,1024]{3,2,1,0:T(1,128)S(1)} %get-tuple-element.79), channel_id=1, source_target_pairs={{0,1},{1,2},{2,3},{3,4},{4,5},{5,6},{6,7},{8,9},{9,10},{10,11},{11... | collective-permute-start | bytes 1658888 | tf_op jit(solution)/shard_map/while/body/eval_jaxpr/ppermute | solution.py:16
  (43 other events, 258.3 us)
Sparse Core Ops, SparseCore 0:
  843.7 22.6 reduce-scatter.1
where the time goes:
time: 887 us; the launch traced here: 884 us
  other arithmetic  300 us (34%)
  waiting for transfers between devices  250 us (28%)
  local copies, waits for them, and re-layouts  233 us (26%)
  starting transfers between devices  69.8 us (8%)
  matrix products  17.6 us (2%)
  between operations  14.1 us (2%)
    add x10, other arithmetic, smooth(): return current + east_side + north_side  171 us
    ppermute x11, waiting for transfers between devices, extended_2(): before = lax.ppermute(last, axis, up)  120 us
    ppermute x11, waiting for transfers between devices, extended_2(): after = lax.ppermute(first, axis, down)  107 us
    mul x10, other arithmetic, smooth(): east_flux = east_weight * (jnp.roll(current, -1, 3) - current)  82.7 us
    slice x20, local copies, waits for them, and re-layouts, smooth(): east_flux = east_weight * (jnp.roll(current, -1, 3) - current)  62 us
    while x100, local copies, waits for them, and re-layouts  60.5 us
    ppermute x11, starting transfers between devices, extended_2(): before = lax.ppermute(last, axis, up)  55.5 us
    slice x10, local copies, waits for them, and re-layouts, extended_2(): first = lax.slice_in_dim(value, 0, width, axis=dim)  48.2 us
  transfers between devices with their start and end apart: 23, of which 21 were waited for; matrix products, arithmetic and copies ran while one was open for 2% of the time, Pallas kernels for 0%

commit v1 on v0

v1 whole, which is shorter than its diff:
```python
import jax
import jax.numpy as jnp
from jax import lax
from jax.experimental import pallas as pl
from jax.experimental.pallas import tpu as pltpu
from jax.sharding import PartitionSpec as P

ITERS = 10
GROUP = 8


def shifted(value, axis, step):
    size = lax.axis_size(axis)
    pairs = [(i, i + step) for i in range(size) if 0 <= i + step < size]
    return lax.ppermute(value, axis, pairs)


def swapped(value, axis):
    size = lax.axis_size(axis)
    return lax.ppermute(value, axis, [(i, i ^ 1) for i in range(size)])


def pair_window(keep, other, odd):
    strip = keep.shape[0]
    lower = jnp.where(odd, other, keep)
    upper = jnp.where(odd, keep, other)
    rest = ITERS - strip
    before = shifted(jnp.concatenate([lower[strip - rest :], upper]), "row", 2)
    after = shifted(jnp.concatenate([lower, upper[:rest]]), "row", -2)
    return lower, upper, before, after


def smooth_kernel(info, stat, keep, other, before, after, own, back, cur, east, north):
    odd, level0 = info[0], info[1]
    strip, count = keep.shape[0], keep.shape[1]
    halo = before.shape[0]
    rows, width = cur.shape[1], cur.shape[3]
    level = (level0 + lax.broadcasted_iota(jnp.int32, (GROUP, width), 0)).astype(jnp.float32)
    mine = halo + strip * odd
    theirs = halo + strip * (1 - odd)

    @pl.loop(0, rows)
    def _(r):
        row = stat[r]
        east[r] = jnp.where(level < row[1:2], row[0:1], 0.0)
        north[r] = jnp.where(level < row[3:4], row[2:3], 0.0)

    def fill(source, start):
        @pl.loop(0, source.shape[0])
        def _(r):
            for f in range(count):
                cur[f, start + r] = source[r, f].astype(jnp.float32)

    fill(before, 0)
    fill(keep, mine)
    fill(other, theirs)
    fill(after, halo + 2 * strip)

    def one_row(f, r, here, south):
        above = cur[f, r + 1]
        north_flux = north[r] * (above - here)
        east_flux = east[r] * (pltpu.roll(here, width - 1, 1) - here)
        east_side = east_flux - pltpu.roll(east_flux, 1, 1)
        cur[f, r] = here + east_side + (north_flux - south)
        return above, north_flux

    @pl.loop(0, count)
    def _(f):
        @pl.loop(0, halo)
        def _(s):
            first = s + 1
            here = cur[f, first]
            south = north[s] * (here - cur[f, s])

            def two_rows(i, carry):
                r = first + 2 * i
                carry = one_row(f, r, *carry)
                return one_row(f, r + 1, *carry)

            lax.fori_loop(0, rows // 2 - 1 - s, two_rows, (here, south))

    @pl.loop(0, strip)
    def _(r):
        for f in range(count):
            own[r, f] = cur[f, mine + r].astype(own.dtype)
            back[r, f] = cur[f, theirs + r].astype(back.dtype)


def smooth(info, stat, keep, other, before, after):
    strip, count, _, width = keep.shape
    rows = 2 * strip + 2 * ITERS
    vmem = pl.BlockSpec(memory_space=pltpu.VMEM)
    steps = (rows - ITERS - 1) * ITERS * count * GROUP * width
    return pl.pallas_call(
        smooth_kernel,
        out_shape=[jax.ShapeDtypeStruct(keep.shape, keep.dtype)] * 2,
        in_specs=[pl.BlockSpec(memory_space=pltpu.SMEM)] + [vmem] * 5,
        out_specs=[vmem] * 2,
        scratch_shapes=[
            pltpu.VMEM((count, rows, GROUP, width), jnp.float32),
            pltpu.VMEM((rows, GROUP, width), jnp.float32),
            pltpu.VMEM((rows, GROUP, width), jnp.float32),
        ],
        compiler_params=pltpu.CompilerParams(vmem_limit_bytes=32 << 20),
        cost_estimate=pl.CostEstimate(
            flops=10 * steps, bytes_accessed=8 << 20, transcendentals=0
        ),
        name="smooth",
    )(info, stat, keep, other, before, after)


def project_kernel(fields, modes, out):
    count, levels, rows, width = fields.shape
    kinds = modes.shape[0]
    for start in range(0, width, 128):
        cols = pl.ds(start, 128)

        def add(l, sums):
            f = [fields[i, l, :, cols].astype(jnp.float32) for i in range(count)]
            new = []
            for k in range(kinds):
                m = modes[k, l, :, cols].astype(jnp.float32)
                new += [sums[k * count + i] + m * f[i] for i in range(count)]
            return tuple(new)

        zero = jnp.zeros((rows, 128), jnp.float32)
        sums = lax.fori_loop(0, levels, add, (zero,) * (count * kinds))
        for k in range(kinds):
            for i in range(count):
                out[0, i, k, :, cols] = sums[k * count + i]


def project(fields, modes, parts):
    count, levels, rows, width = fields.shape
    kinds = modes.shape[0]
    tile = 256
    per = width // parts // tile
    return pl.pallas_call(
        project_kernel,
        grid=(parts * per,),
        out_shape=jax.ShapeDtypeStruct((parts, count, kinds, rows, width // parts), jnp.float32),
        in_specs=[
            pl.BlockSpec((count, levels, rows, tile), lambda j: (0, 0, 0, j)),
            pl.BlockSpec((kinds, levels, rows, tile), lambda j: (0, 0, 0, j)),
        ],
        out_specs=pl.BlockSpec(
            (1, count, kinds, rows, tile), lambda j: (j // per, 0, 0, 0, j % per)
        ),
        compiler_params=pltpu.CompilerParams(vmem_limit_bytes=32 << 20),
        cost_estimate=pl.CostEstimate(
            flops=2 * count * kinds * levels * rows * width,
            bytes_accessed=2 * (count + kinds) * levels * rows * width,
            transcendentals=0,
        ),
        name="project",
    )(fields, modes)


def per_device(fields, vertical_modes, diffusivity, land_mask, wet_levels):
    levels = fields.shape[1]
    strip = fields.shape[2]
    odd = lax.axis_index("row") % 2 == 1
    groups = -(-(levels + 1) // 2 // GROUP)
    span = groups * GROUP
    top = levels - span

    depth = (land_mask * wet_levels).astype(jnp.float32)
    statics = jnp.stack([diffusivity, depth], axis=1)
    lower, upper, before, after = pair_window(statics, swapped(statics, "row"), odd)
    whole = jnp.concatenate([before, lower, upper, after])
    diff, deep = whole[:, 0], whole[:, 1]
    east = 0.5 * (diff + jnp.roll(diff, -1, 1))
    is_last = jnp.arange(diff.shape[1]) == diff.shape[1] - 1
    east_deep = jnp.where(is_last[None], 0.0, jnp.minimum(deep, jnp.roll(deep, -1, 1)))
    north = 0.5 * (diff + jnp.roll(diff, -1, 0))
    north_deep = jnp.minimum(deep, jnp.roll(deep, -1, 0))
    stat = jnp.stack([east, east_deep, north, north_deep], axis=1)

    by_row = jnp.transpose(fields, (2, 0, 1, 3))
    start = lax.axis_index("lev") * levels + jnp.where(odd, top, 0)
    kept, returned = [], []
    last = None
    for g in range(groups):
        low = by_row[:, :, g * GROUP : (g + 1) * GROUP]
        high = by_row[:, :, top + g * GROUP : top + (g + 1) * GROUP]
        keep = jnp.where(odd, high, low)
        give = jnp.where(odd, low, high)
        if last is not None:
            give, last = lax.optimization_barrier((give, last))
        other = last = swapped(give, "row")
        _, _, before, after = pair_window(keep, other, odd)
        info = jnp.stack([odd.astype(jnp.int32), (start + g * GROUP).astype(jnp.int32)])
        own, back = smooth(info, stat, keep, other, before, after)
        kept.append(own)
        returned.append(swapped(back, "row"))
    kept, returned = jnp.concatenate(kept, 2), jnp.concatenate(returned, 2)
    low = jnp.where(odd, returned, kept)
    high = jnp.where(odd, kept, returned)
    filtered = jnp.concatenate([low, high[:, :, span - top :]], axis=2)
    filtered = jnp.transpose(filtered, (1, 2, 0, 3))

    parts = lax.axis_size("lev")
    terms = project(filtered, vertical_modes, parts)
    here = lax.axis_index("lev")
    amplitude = lax.dynamic_index_in_dim(terms, here, 0, keepdims=False)
    for step in range(1, parts):
        away = lax.dynamic_index_in_dim(terms, (here + step) % parts, 0, keepdims=False)
        ring = [(i, (i + step) % parts) for i in range(parts)]
        amplitude = amplitude + lax.ppermute(away, "lev", ring)
    modal_flux = jnp.stack(
        [
            amplitude[0] * amplitude[2],
            amplitude[1] * amplitude[2],
            0.5 * (amplitude[0] * amplitude[0] + amplitude[1] * amplitude[1]),
        ]
    )
    return (filtered, modal_flux)


def solution(mesh):
    placed = (
        P("group", "lev", "row", None),
        P(None, "lev", "row", None),
        P("row", None),
        P("row", None),
        P("row", None),
    )
    return jax.shard_map(
        per_device,
        mesh=mesh,
        in_specs=placed,
        out_specs=(P("group", "lev", "row", None), P("group", None, "row", "lev")),
        check_vma=False,
    )
```

time: 887 us -> 290 us (0.33)
  other arithmetic: 300 us -> 5.91 us
  local copies, waits for them, and re-layouts: 233 us -> 6.74 us
  waiting for transfers between devices: 250 us -> 52 us
  Pallas kernels: 0 us -> 191 us
  starting transfers between devices: 69.8 us -> 32.1 us
  matrix products: 17.6 us -> 0 us
  between operations: 14.1 us -> 1.24 us
    pallas_call x0 -> x4, Pallas kernels: none -> 191 us  [the longest x3 185 us: smooth(): pl.pallas_call(smooth_kernel, out_shape=[jax.ShapeDtypeStruct(keep.shape,...]
    ppermute x22 -> x16, waiting for transfers between devices: 227 us -> 52 us  [the longest x7 32.4 us: swapped(): return lax.ppermute(value, axis, [(i, i ^ 1) for i in range(size)])]
    add x11 -> x1, other arithmetic: 171 us -> 0.06 us  [per_device(): amplitude = amplitude + lax.ppermute(away, 'lev', ring)]
    slice x51 -> x15, local copies, waits for them, and re-layouts: 125 us -> 0.93 us  [the longest x1 0.23 us: per_device(): diff, deep = (whole[:, 0], whole[:, 1])]
    mul x14 -> x1, other arithmetic: 84.4 us -> 0.75 us  [per_device(): east = 0.5 * (diff + jnp.roll(diff, -1, 1))]
    while x100 -> x0, local copies, waits for them, and re-layouts: 60.5 us -> none
    ppermute x22 -> x16, starting transfers between devices: 69.7 us -> 32.1 us  [the longest x8 22.1 us: shifted(): return lax.ppermute(value, axis, pairs)]
    concatenate x10 -> x9, other arithmetic: 34.5 us -> 1.12 us  [the longest x4 0.81 us: pair_window(): after = shifted(jnp.concatenate([lower, upper[:rest]]), 'row', -2)]
  transfers between devices with their start and end apart: 23 -> 16, of which waited for: 21 -> 8; matrix products, arithmetic and copies ran while one was open for 2% -> 2% of each run, Pallas kernels for 0% -> 64%
where the time goes in v1:
time: 290 us; the launch traced here: 289 us
  Pallas kernels  191 us (66%)
  waiting for transfers between devices  52 us (18%)
  starting transfers between devices  32.1 us (11%)
  local copies, waits for them, and re-layouts  6.74 us (2%)
  other arithmetic  5.91 us (2%)
    pallas_call x3, Pallas kernels, smooth(): pl.pallas_call(smooth_kernel, out_shape=[jax.ShapeDtypeStruct(keep.shape,...  185 us
    ppermute x7, waiting for transfers between devices, swapped(): return lax.ppermute(value, axis, [(i, i ^ 1) for i in range(size)])  32.4 us
    ppermute x8, starting transfers between devices, shifted(): return lax.ppermute(value, axis, pairs)  22.1 us
    ppermute x8, waiting for transfers between devices, shifted(): return lax.ppermute(value, axis, pairs)  17.9 us
    ppermute x7, starting transfers between devices, swapped(): return lax.ppermute(value, axis, [(i, i ^ 1) for i in range(size)])  9.89 us
    pallas_call x1, Pallas kernels, project(): pl.pallas_call(project_kernel, grid=(parts * per,), out_shape=jax.ShapeDt...  6.53 us
  transfers between devices with their start and end apart: 16, of which 8 were waited for; matrix products, arithmetic and copies ran while one was open for 2% of the time, Pallas kernels for 64%

profile of v1, /device:TPU:0, one launch (start us, length us, event | category | flops | bytes accessed | tf_op | source)
XLA Modules:
  0.0 289.2 jit_solution(16812727111708902247)
XLA Ops:
  0.6 2.8 copy.39
  3.5 1.2 broadcast_select_fusion.3
  4.7 3.0 %collective-permute-start.3 = (bf16[8,3,8,1024]{3,2,1,0:T(8,128)(2,1)}, bf16[8,3,8,1024]{3,2,1,0:T(8,128)(2,1)S(1)}, u32[]{:S(2)}, u32[]{:S(2)}) collective-permute-start(bf16[8,3,8,1024]{3,2,1,0:T(8,128)(2,1)} %get-tuple-element.29), channel_id=1, source_target_pairs={{0,1},{1,0},{2,3},{3,2},{4,5},{5,4},{6,7},{7,6},{8,9},{9,8},{10,11... | collective-permute-start | bytes 1179656 | tf_op jit(solution)/shard_map/ppermute | solution.py:20
  8.1 10.3 %collective-permute-done = f32[8,2,1024]{2,1,0:T(2,128)S(1)} collective-permute-done((f32[8,2,1024]{2,1,0:T(2,128)S(1)}, f32[8,2,1024]{2,1,0:T(2,128)S(1)}, u32[]{:S(2)}, u32[]{:S(2)}) %collective-permute-start) | collective-permute-done | bytes 65568 | tf_op jit(solution)/shard_map/ppermute | solution.py:20
  18.6 3.7 %collective-permute-start.1 = (f32[10,2,1024]{2,1,0:T(2,128)S(1)}, f32[10,2,1024]{2,1,0:T(2,128)S(1)}, u32[]{:S(2)}, u32[]{:S(2)}) collective-permute-start(f32[10,2,1024]{2,1,0:T(2,128)S(1)} %pad_maximum_fusion.9), channel_id=1, source_target_pairs={{0,2},{1,3},{2,4},{3,5},{4,6},{5,7},{8,10},{9,11},{10,12},{11,13},... | collective-permute-start | bytes 245768 | tf_op jit(solution)/shard_map/ppermute | solution.py:15
  22.3 0.7 pad_maximum_fusion.10
  23.0 1.3 collective-permute-start.2
  24.4 5.2 %collective-permute-done.2 = f32[10,2,1024]{2,1,0:T(2,128)S(1)} collective-permute-done((f32[10,2,1024]{2,1,0:T(2,128)}, f32[10,2,1024]{2,1,0:T(2,128)S(1)}, u32[]{:S(2)}, u32[]{:S(2)}) %collective-permute-start.2) | collective-permute-done | bytes 81952 | tf_op jit(solution)/shard_map/ppermute | solution.py:15
  29.9 1.6 collective-permute-start.7
  32.4 6.8 %collective-permute-done.7.other = bf16[8,3,8,1024]{3,2,1,0:T(8,128)(2,1)S(1)} collective-permute-done((bf16[8,3,8,1024]{3,2,1,0:T(8,128)(2,1)S(1)}, bf16[8,3,8,1024]{3,2,1,0:T(8,128)(2,1)S(1)}, u32[]{:S(2)}, u32[]{:S(2)}) %collective-permute-start.7) | collective-permute-done | bytes 393248 | tf_op jit(solution)/shard_map/ppermute | solution.py:20
  39.3 1.5 collective-permute-start.11
  41.0 6.0 %collective-permute-done.11.other = bf16[8,3,8,1024]{3,2,1,0:T(8,128)(2,1)S(1)} collective-permute-done((bf16[8,3,8,1024]{3,2,1,0:T(8,128)(2,1)S(1)}, bf16[8,3,8,1024]{3,2,1,0:T(8,128)(2,1)S(1)}, u32[]{:S(2)}, u32[]{:S(2)}) %collective-permute-start.11) | collective-permute-done | bytes 393248 | tf_op jit(solution)/shard_map/ppermute | solution.py:20
  47.6 1.3 collective-permute-start.9
  49.1 1.3 collective-permute-start.13
  50.5 1.3 collective-permute-start.5
  51.8 5.8 %collective-permute-start.4 = (bf16[10,3,8,1024]{3,2,1,0:T(8,128)(2,1)S(1)}, bf16[10,3,8,1024]{3,2,1,0:T(8,128)(2,1)S(1)}, u32[]{:S(2)}, u32[]{:S(2)}) collective-permute-start(bf16[10,3,8,1024]{3,2,1,0:T(8,128)(2,1)S(1)} %pad_maximum_fusion.1), channel_id=1, source_target_pairs={{0,2},{1,3},{2,4},{3,5},{4,6},{5,7},{8,10},{9,11},{10,12},{11,13},... | collective-permute-start | bytes 1474568 | tf_op jit(solution)/shard_map/ppermute | solution.py:15
  57.7 3.9 %collective-permute-start.12 = (bf16[10,3,8,1024]{3,2,1,0:T(8,128)(2,1)S(1)}, bf16[10,3,8,1024]{3,2,1,0:T(8,128)(2,1)S(1)}, u32[]{:S(2)}, u32[]{:S(2)}) collective-permute-start(bf16[10,3,8,1024]{3,2,1,0:T(8,128)(2,1)S(1)} %pad_maximum_fusion.5), channel_id=1, source_target_pairs={{0,2},{1,3},{2,4},{3,5},{4,6},{5,7},{8,10},{9,11},{10,12},{11,13},... | collective-permute-start | bytes 1474568 | tf_op jit(solution)/shard_map/ppermute | solution.py:15
  61.7 12.2 %collective-permute-done.13.after = bf16[10,3,8,1024]{3,2,1,0:T(8,128)(2,1)S(1)} collective-permute-done((bf16[10,3,8,1024]{3,2,1,0:T(8,128)(2,1)S(1)}, bf16[10,3,8,1024]{3,2,1,0:T(8,128)(2,1)S(1)}, u32[]{:S(2)}, u32[]{:S(2)}) %collective-permute-start.13) | collective-permute-done | bytes 491552 | tf_op jit(solution)/shard_map/ppermute | solution.py:15
  73.9 3.5 %collective-permute-start.8 = (bf16[10,3,8,1024]{3,2,1,0:T(8,128)(2,1)S(1)}, bf16[10,3,8,1024]{3,2,1,0:T(8,128)(2,1)S(1)}, u32[]{:S(2)}, u32[]{:S(2)}) collective-permute-start(bf16[10,3,8,1024]{3,2,1,0:T(8,128)(2,1)S(1)} %pad_maximum_fusion.3), channel_id=1, source_target_pairs={{0,2},{1,3},{2,4},{3,5},{4,6},{5,7},{8,10},{9,11},{10,12},{11,13},... | collective-permute-start | bytes 1474568 | tf_op jit(solution)/shard_map/ppermute | solution.py:15
  77.4 0.8 fusion
  78.2 0.6 pad_maximum_fusion.stat
  79.3 61.5 %smooth.5 = (bf16[8,3,8,1024]{3,2,1,0:T(8,128)(2,1)S(1)}, bf16[8,3,8,1024]{3,2,1,0:T(8,128)(2,1)S(1)}) custom-call(s32[2]{0:T(128)S(1)} %pad_add_fusion.2.info, f32[36,4,1024]{2,1,0:T(4,128)S(1)} %pad_maximum_fusion.stat, bf16[8,3,8,1024]{3,2,1,0:T(8,128)(2,1)S(1)} %get-tuple-element.19.keep, bf16[8,3,8,1024]{3,2,1,0:T(8,128)(2,1)S(1)} %collective-permute-done.11.other, ...), custom_call_target="tpu_custom_call" | custom-call | flops 61440000 | bytes 8388608 | tf_op jit(solution)/shard_map/smooth/pallas_call | solution.py:94
  141.1 1.6 collective-permute-start.14
  142.7 61.5 %smooth.3 = (bf16[8,3,8,1024]{3,2,1,0:T(8,128)(2,1)S(1)}, bf16[8,3,8,1024]{3,2,1,0:T(8,128)(2,1)S(1)}) custom-call(s32[2]{0:T(128)S(1)} %pad_add_fusion.info, f32[36,4,1024]{2,1,0:T(4,128)S(1)} %pad_maximum_fusion.stat, bf16[8,3,8,1024]{3,2,1,0:T(8,128)(2,1)S(1)} %get-tuple-element.27.keep, bf16[8,3,8,1024]{3,2,1,0:T(8,128)(2,1)S(1)} %collective-permute-done.3.other, ...), custom_call_target="tpu_custom_call" | custom-call | flops 61440000 | bytes 8388608 | tf_op jit(solution)/shard_map/smooth/pallas_call | solution.py:94
  204.5 61.6 %smooth.4 = (bf16[8,3,8,1024]{3,2,1,0:T(8,128)(2,1)S(1)}, bf16[8,3,8,1024]{3,2,1,0:T(8,128)(2,1)S(1)}) custom-call(s32[2]{0:T(128)S(1)} %pad_add_fusion.1.info, f32[36,4,1024]{2,1,0:T(4,128)S(1)} %pad_maximum_fusion.stat, bf16[8,3,8,1024]{3,2,1,0:T(8,128)(2,1)S(1)} %get-tuple-element.25.keep, bf16[8,3,8,1024]{3,2,1,0:T(8,128)(2,1)S(1)} %collective-permute-done.7.other, ...), custom_call_target="tpu_custom_call" | custom-call | flops 61440000 | bytes 8388608 | tf_op jit(solution)/shard_map/smooth/pallas_call | solution.py:94
  266.3 0.6 collective-permute-start.10
  267.1 1.6 collective-permute-start.6
  269.1 9.2 %collective-permute-done.6 = bf16[8,3,8,1024]{3,0,2,1:T(8,128)(2,1)S(1)} collective-permute-done((bf16[8,3,8,1024]{3,0,2,1:T(8,128)(2,1)S(1)}, bf16[8,3,8,1024]{3,0,2,1:T(8,128)(2,1)S(1)}, u32[]{:S(2)}, u32[]{:S(2)}) %collective-permute-start.6) | collective-permute-done | bytes 393248 | tf_op jit(solution)/shard_map/ppermute | solution.py:20
  279.0 1.0 slice-done.1
  279.9 6.5 %project.1 = f32[2,3,8,8,512]{4,3,2,1,0:T(8,128)S(1)} custom-call(bf16[3,45,8,1024]{3,2,1,0:T(8,128)(2,1)S(1)} %maximum_bitcast_fusion.fields, bf16[8,45,8,1024]{3,2,1,0:T(8,128)(2,1)S(1)} %bitcast.18), custom_call_target="tpu_custom_call" | custom-call | flops 17694720 | bytes 8110080 | tf_op jit(solution)/shard_map/project/pallas_call | solution.py:138
  286.6 1.7 collective-permute-done.15
  288.4 0.8 pad_maximum_fusion.7
  (81 shorter events, 5.6 us)
Async XLA Ops:
  3.5 4.2 %copy-start.2 = (s32[8,1024]{1,0:T(8,128)S(1)}, s32[8,1024]{1,0:T(8,128)}, u32[]{:S(2)}) copy-start(s32[8,1024]{1,0:T(8,128)} %param.8) | copy-start | bytes 98308
  3.5 4.2 %copy-start.3 = (s32[8,1024]{1,0:T(8,128)S(1)}, s32[8,1024]{1,0:T(8,128)}, u32[]{:S(2)}) copy-start(s32[8,1024]{1,0:T(8,128)} %param.9) | copy-start | bytes 98308
  3.5 4.3 %copy-start.4 = (f32[8,1024]{1,0:T(8,128)S(1)}, f32[8,1024]{1,0:T(8,128)}, u32[]{:S(2)}) copy-start(f32[8,1024]{1,0:T(8,128)} %param.7) | copy-start | bytes 98308
  4.7 25.1 %collective-permute-start.3 = (bf16[8,3,8,1024]{3,2,1,0:T(8,128)(2,1)}, bf16[8,3,8,1024]{3,2,1,0:T(8,128)(2,1)S(1)}, u32[]{:S(2)}, u32[]{:S(2)}) collective-permute-start(bf16[8,3,8,1024]{3,2,1,0:T(8,128)(2,1)} %get-tuple-element.29), channel_id=1, source_target_pairs={{0,1},{1,0},{2,3},{3,2},{4,5},{5,4},{6,7},{7,6},{8,9},{9,8},{10,11... | collective-permute-start | bytes 1179656 | tf_op jit(solution)/shard_map/ppermute | solution.py:20
  7.9 10.6 %collective-permute-start = (f32[8,2,1024]{2,1,0:T(2,128)S(1)}, f32[8,2,1024]{2,1,0:T(2,128)S(1)}, u32[]{:S(2)}, u32[]{:S(2)}) collective-permute-start(f32[8,2,1024]{2,1,0:T(2,128)S(1)} %pad_maximum_fusion.11), channel_id=1, source_target_pairs={{0,1},{1,0},{2,3},{3,2},{4,5},{5,4},{6,7},{7,6},{8,9},{9,8},{10,11... | collective-permute-start | bytes 196616 | tf_op jit(solution)/shard_map/ppermute | solution.py:20
  18.6 5.8 %collective-permute-start.1 = (f32[10,2,1024]{2,1,0:T(2,128)S(1)}, f32[10,2,1024]{2,1,0:T(2,128)S(1)}, u32[]{:S(2)}, u32[]{:S(2)}) collective-permute-start(f32[10,2,1024]{2,1,0:T(2,128)S(1)} %pad_maximum_fusion.9), channel_id=1, source_target_pairs={{0,2},{1,3},{2,4},{3,5},{4,6},{5,7},{8,10},{9,11},{10,12},{11,13},... | collective-permute-start | bytes 245768 | tf_op jit(solution)/shard_map/ppermute | solution.py:15
  23.0 6.5 %collective-permute-start.2 = (f32[10,2,1024]{2,1,0:T(2,128)}, f32[10,2,1024]{2,1,0:T(2,128)S(1)}, u32[]{:S(2)}, u32[]{:S(2)}) collective-permute-start(f32[10,2,1024]{2,1,0:T(2,128)} %pad_maximum_fusion.10), channel_id=1, source_target_pairs={{2,0},{3,1},{4,2},{5,3},{6,4},{7,5},{10,8},{11,9},{12,10},{13,11},... | collective-permute-start | bytes 245768 | tf_op jit(solution)/shard_map/ppermute | solution.py:15
  24.4 5.5 %copy-start.1 = (bf16[8,3,8,1024]{3,2,1,0:T(8,128)(2,1)S(1)}, bf16[8,3,8,1024]{3,2,1,0:T(8,128)(2,1)}, u32[]{:S(2)}) copy-start(bf16[8,3,8,1024]{3,2,1,0:T(8,128)(2,1)} %get-tuple-element.11) | copy-start | bytes 1179652
  29.9 9.3 %collective-permute-start.7 = (bf16[8,3,8,1024]{3,2,1,0:T(8,128)(2,1)S(1)}, bf16[8,3,8,1024]{3,2,1,0:T(8,128)(2,1)S(1)}, u32[]{:S(2)}, u32[]{:S(2)}) collective-permute-start(bf16[8,3,8,1024]{3,2,1,0:T(8,128)(2,1)S(1)} %copy-done.1), channel_id=1, source_target_pairs={{0,1},{1,0},{2,3},{3,2},{4,5},{5,4},{6,7},{7,6},{8,9},{9,8},{10,11... | collective-permute-start | bytes 1179656 | tf_op jit(solution)/shard_map/ppermute | solution.py:20
  39.3 7.8 %collective-permute-start.11 = (bf16[8,3,8,1024]{3,2,1,0:T(8,128)(2,1)S(1)}, bf16[8,3,8,1024]{3,2,1,0:T(8,128)(2,1)S(1)}, u32[]{:S(2)}, u32[]{:S(2)}) collective-permute-start(bf16[8,3,8,1024]{3,2,1,0:T(8,128)(2,1)S(1)} %get-tuple-element.13), channel_id=1, source_target_pairs={{0,1},{1,0},{2,3},{3,2},{4,5},{5,4},{6,7},{7,6},{8,9},{9,8},{10,11... | collective-permute-start | bytes 1179656 | tf_op jit(solution)/shard_map/ppermute | solution.py:20
  47.6 156.9 %collective-permute-start.9 = (bf16[10,3,8,1024]{3,2,1,0:T(8,128)(2,1)S(1)}, bf16[10,3,8,1024]{3,2,1,0:T(8,128)(2,1)S(1)}, u32[]{:S(2)}, u32[]{:S(2)}) collective-permute-start(bf16[10,3,8,1024]{3,2,1,0:T(8,128)(2,1)S(1)} %pad_maximum_fusion.4), channel_id=1, source_target_pairs={{2,0},{3,1},{4,2},{5,3},{6,4},{7,5},{10,8},{11,9},{12,10},{13,11},... | collective-permute-start | bytes 1474568 | tf_op jit(solution)/shard_map/ppermute | solution.py:15
  49.1 24.8 %collective-permute-start.13 = (bf16[10,3,8,1024]{3,2,1,0:T(8,128)(2,1)S(1)}, bf16[10,3,8,1024]{3,2,1,0:T(8,128)(2,1)S(1)}, u32[]{:S(2)}, u32[]{:S(2)}) collective-permute-start(bf16[10,3,8,1024]{3,2,1,0:T(8,128)(2,1)S(1)} %pad_maximum_fusion.6), channel_id=1, source_target_pairs={{2,0},{3,1},{4,2},{5,3},{6,4},{7,5},{10,8},{11,9},{12,10},{13,11},... | collective-permute-start | bytes 1474568 | tf_op jit(solution)/shard_map/ppermute | solution.py:15
  50.5 92.2 %collective-permute-start.5 = (bf16[10,3,8,1024]{3,2,1,0:T(8,128)(2,1)S(1)}, bf16[10,3,8,1024]{3,2,1,0:T(8,128)(2,1)S(1)}, u32[]{:S(2)}, u32[]{:S(2)}) collective-permute-start(bf16[10,3,8,1024]{3,2,1,0:T(8,128)(2,1)S(1)} %pad_maximum_fusion.2), channel_id=1, source_target_pairs={{2,0},{3,1},{4,2},{5,3},{6,4},{7,5},{10,8},{11,9},{12,10},{13,11},... | collective-permute-start | bytes 1474568 | tf_op jit(solution)/shard_map/ppermute | solution.py:15
  51.8 90.9 %collective-permute-start.4 = (bf16[10,3,8,1024]{3,2,1,0:T(8,128)(2,1)S(1)}, bf16[10,3,8,1024]{3,2,1,0:T(8,128)(2,1)S(1)}, u32[]{:S(2)}, u32[]{:S(2)}) collective-permute-start(bf16[10,3,8,1024]{3,2,1,0:T(8,128)(2,1)S(1)} %pad_maximum_fusion.1), channel_id=1, source_target_pairs={{0,2},{1,3},{2,4},{3,5},{4,6},{5,7},{8,10},{9,11},{10,12},{11,13},... | collective-permute-start | bytes 1474568 | tf_op jit(solution)/shard_map/ppermute | solution.py:15
  57.7 21.6 %collective-permute-start.12 = (bf16[10,3,8,1024]{3,2,1,0:T(8,128)(2,1)S(1)}, bf16[10,3,8,1024]{3,2,1,0:T(8,128)(2,1)S(1)}, u32[]{:S(2)}, u32[]{:S(2)}) collective-permute-start(bf16[10,3,8,1024]{3,2,1,0:T(8,128)(2,1)S(1)} %pad_maximum_fusion.5), channel_id=1, source_target_pairs={{0,2},{1,3},{2,4},{3,5},{4,6},{5,7},{8,10},{9,11},{10,12},{11,13},... | collective-permute-start | bytes 1474568 | tf_op jit(solution)/shard_map/ppermute | solution.py:15
  73.9 130.5 %collective-permute-start.8 = (bf16[10,3,8,1024]{3,2,1,0:T(8,128)(2,1)S(1)}, bf16[10,3,8,1024]{3,2,1,0:T(8,128)(2,1)S(1)}, u32[]{:S(2)}, u32[]{:S(2)}) collective-permute-start(bf16[10,3,8,1024]{3,2,1,0:T(8,128)(2,1)S(1)} %pad_maximum_fusion.3), channel_id=1, source_target_pairs={{0,2},{1,3},{2,4},{3,5},{4,6},{5,7},{8,10},{9,11},{10,12},{11,13},... | collective-permute-start | bytes 1474568 | tf_op jit(solution)/shard_map/ppermute | solution.py:15
  141.1 137.3 %collective-permute-start.14 = (bf16[8,3,8,1024]{3,0,2,1:T(8,128)(2,1)S(1)}, bf16[8,3,8,1024]{3,0,2,1:T(8,128)(2,1)S(1)}, u32[]{:S(2)}, u32[]{:S(2)}) collective-permute-start(bf16[8,3,8,1024]{3,0,2,1:T(8,128)(2,1)S(1)} %copy.27), channel_id=1, source_target_pairs={{0,1},{1,0},{2,3},{3,2},{4,5},{5,4},{6,7},{7,6},{8,9},{9,8},{10,11... | collective-permute-start | bytes 1179656 | tf_op jit(solution)/shard_map/ppermute | solution.py:20
  266.3 12.1 %collective-permute-start.10 = (bf16[8,3,8,1024]{3,0,2,1:T(8,128)(2,1)S(1)}, bf16[8,3,8,1024]{3,0,2,1:T(8,128)(2,1)S(1)}, u32[]{:S(2)}, u32[]{:S(2)}) collective-permute-start(bf16[8,3,8,1024]{3,0,2,1:T(8,128)(2,1)S(1)} %copy.26), channel_id=1, source_target_pairs={{0,1},{1,0},{2,3},{3,2},{4,5},{5,4},{6,7},{7,6},{8,9},{9,8},{10,11... | collective-permute-start | bytes 1179656 | tf_op jit(solution)/shard_map/ppermute | solution.py:20
  266.8 12.1 %slice-start = ((s8[5898240]{0:T(1024)(128)(4,1)}), s8[4194304]{0:T(1024)(128)(4,1)S(1)}, s32[]{:S(2)}) async-start(s8[5898240]{0:T(1024)(128)(4,1)} %bitcast.17), calls=%async_computation | async-start | bytes 8388608
  267.1 11.3 %collective-permute-start.6 = (bf16[8,3,8,1024]{3,0,2,1:T(8,128)(2,1)S(1)}, bf16[8,3,8,1024]{3,0,2,1:T(8,128)(2,1)S(1)}, u32[]{:S(2)}, u32[]{:S(2)}) collective-permute-start(bf16[8,3,8,1024]{3,0,2,1:T(8,128)(2,1)S(1)} %copy.25), channel_id=1, source_target_pairs={{0,1},{1,0},{2,3},{3,2},{4,5},{5,4},{6,7},{7,6},{8,9},{9,8},{10,11... | collective-permute-start | bytes 1179656 | tf_op jit(solution)/shard_map/ppermute | solution.py:20
  278.5 1.5 slice-start.1
  279.9 6.5 %copy-start = (bf16[3,45,8,1024]{3,2,1,0:T(8,128)(2,1)}, bf16[3,45,8,1024]{3,2,1,0:T(8,128)(2,1)S(1)}, u32[]{:S(2)}) copy-start(bf16[3,45,8,1024]{3,2,1,0:T(8,128)(2,1)S(1)} %maximum_bitcast_fusion.fields) | copy-start | bytes 6635524
  286.5 1.8 collective-permute-start.15

commit v2 on v1

--- a/solution.py
+++ b/solution.py
@@ -30,7 +30,7 @@
     return lower, upper, before, after
 
 
-def smooth_kernel(info, stat, keep, other, before, after, own, back, cur, east, north):
+def smooth_kernel(info, stat, keep, other, before, after, own, back, cur, nxt, east, west, north):
     odd, level0 = info[0], info[1]
     strip, count = keep.shape[0], keep.shape[1]
     halo = before.shape[0]
@@ -43,6 +43,7 @@
     def _(r):
         row = stat[r]
         east[r] = jnp.where(level < row[1:2], row[0:1], 0.0)
+        west[r] = pltpu.roll(east[r], 1, 1)
         north[r] = jnp.where(level < row[3:4], row[2:3], 0.0)
 
     def fill(source, start):
@@ -56,28 +57,23 @@
     fill(other, theirs)
     fill(after, halo + 2 * strip)
 
-    def one_row(f, r, here, south):
-        above = cur[f, r + 1]
-        north_flux = north[r] * (above - here)
-        east_flux = east[r] * (pltpu.roll(here, width - 1, 1) - here)
-        east_side = east_flux - pltpu.roll(east_flux, 1, 1)
-        cur[f, r] = here + east_side + (north_flux - south)
-        return above, north_flux
-
-    @pl.loop(0, count)
-    def _(f):
-        @pl.loop(0, halo)
-        def _(s):
-            first = s + 1
-            here = cur[f, first]
-            south = north[s] * (here - cur[f, s])
-
-            def two_rows(i, carry):
-                r = first + 2 * i
-                carry = one_row(f, r, *carry)
-                return one_row(f, r + 1, *carry)
-
-            lax.fori_loop(0, rows // 2 - 1 - s, two_rows, (here, south))
+    def one_step(source, target, s):
+        @pl.loop(0, rows // 2 - 1 - s)
+        def _(i):
+            r = s + 1 + 2 * i
+            for f in range(count):
+                held = [source[f, r + d] for d in range(-1, 3)]
+                side = [north[r - 1 + d] * (held[d + 1] - held[d]) for d in range(3)]
+                for d in range(2):
+                    here = held[d + 1]
+                    east_flux = east[r + d] * (pltpu.roll(here, width - 1, 1) - here)
+                    west_flux = west[r + d] * (here - pltpu.roll(here, 1, 1))
+                    target[f, r + d] = here + (east_flux - west_flux) + (side[d + 1] - side[d])
+
+    @pl.loop(0, halo // 2)
+    def _(j):
+        one_step(cur, nxt, 2 * j)
+        one_step(nxt, cur, 2 * j + 1)
 
     @pl.loop(0, strip)
     def _(r):
@@ -98,6 +94,8 @@
         out_specs=[vmem] * 2,
         scratch_shapes=[
             pltpu.VMEM((count, rows, GROUP, width), jnp.float32),
+            pltpu.VMEM((count, rows, GROUP, width), jnp.float32),
+            pltpu.VMEM((rows, GROUP, width), jnp.float32),
             pltpu.VMEM((rows, GROUP, width), jnp.float32),
             pltpu.VMEM((rows, GROUP, width), jnp.float32),
         ],
@@ -179,15 +177,12 @@
     by_row = jnp.transpose(fields, (2, 0, 1, 3))
     start = lax.axis_index("lev") * levels + jnp.where(odd, top, 0)
     kept, returned = [], []
-    last = None
     for g in range(groups):
         low = by_row[:, :, g * GROUP : (g + 1) * GROUP]
         high = by_row[:, :, top + g * GROUP : top + (g + 1) * GROUP]
         keep = jnp.where(odd, high, low)
         give = jnp.where(odd, low, high)
-        if last is not None:
-            give, last = lax.optimization_barrier((give, last))
-        other = last = swapped(give, "row")
+        other = swapped(give, "row")
         _, _, before, after = pair_window(keep, other, odd)
         info = jnp.stack([odd.astype(jnp.int32), (start + g * GROUP).astype(jnp.int32)])
         own, back = smooth(info, stat, keep, other, before, after)

time: 290 us -> 166 us (0.57)
  Pallas kernels: 191 us -> 83.8 us
  waiting for transfers between devices: 52 us -> 38.1 us
    pallas_call x3, Pallas kernels: 185 us -> 77.2 us  [smooth(): pl.pallas_call(smooth_kernel, out_shape=[jax.ShapeDtypeStruct(keep.shape,...]
    ppermute x8, waiting for transfers between devices: 17.9 us -> 4.97 us  [shifted(): return lax.ppermute(value, axis, pairs)]
  transfers between devices with their start and end apart: 16 -> 16, of which waited for: 8 -> 7; matrix products, arithmetic and copies ran while one was open for 2% -> 3% of each run, Pallas kernels for 64% -> 47%
where the time goes in v2:
time: 166 us; the launch traced here: 165 us
  Pallas kernels  83.8 us (50%)
  waiting for transfers between devices  38.1 us (23%)
  starting transfers between devices  31 us (19%)
  local copies, waits for them, and re-layouts  6.73 us (4%)
  other arithmetic  4.41 us (3%)
    pallas_call x3, Pallas kernels, smooth(): pl.pallas_call(smooth_kernel, out_shape=[jax.ShapeDtypeStruct(keep.shape,...  77.2 us
    ppermute x7, waiting for transfers between devices, swapped(): return lax.ppermute(value, axis, [(i, i ^ 1) for i in range(size)])  31.5 us
    ppermute x8, starting transfers between devices, shifted(): return lax.ppermute(value, axis, pairs)  21.5 us
    ppermute x7, starting transfers between devices, swapped(): return lax.ppermute(value, axis, [(i, i ^ 1) for i in range(size)])  9.45 us
    pallas_call x1, Pallas kernels, project(): pl.pallas_call(project_kernel, grid=(parts * per,), out_shape=jax.ShapeDt...  6.53 us
    ppermute x8, waiting for transfers between devices, shifted(): return lax.ppermute(value, axis, pairs)  4.97 us
    unnamed x17, local copies, waits for them, and re-layouts  4.33 us
  transfers between devices with their start and end apart: 16, of which 7 were waited for; matrix products, arithmetic and copies ran while one was open for 3% of the time, Pallas kernels for 47%

profile of v2, /device:TPU:0, one launch (start us, length us, event | category | flops | bytes accessed | tf_op | source)
XLA Modules:
  0.0 165.4 jit_solution(1537224921103560502)
XLA Ops:
  0.6 2.8 %copy.39 = bf16[3,45,8,1024]{3,1,0,2:T(8,128)(2,1)S(1)} copy(bf16[3,45,8,1024]{3,2,1,0:T(8,128)(2,1)} %param.5) | data formatting | bytes 4423680 | tf_op args[0]
  3.7 3.0 %collective-permute-start.11 = (bf16[8,3,8,1024]{3,2,1,0:T(8,128)(2,1)S(1)}, bf16[8,3,8,1024]{3,2,1,0:T(8,128)(2,1)S(1)}, u32[]{:S(2)}, u32[]{:S(2)}) collective-permute-start(bf16[8,3,8,1024]{3,2,1,0:T(8,128)(2,1)S(1)} %broadcast_select_fusion.3), channel_id=1, source_target_pairs={{0,1},{1,0},{2,3},{3,2},{4,5},{5,4},{6,7},{7,6},{8,9},{9,8},{10,11... | collective-permute-start | bytes 1179656 | tf_op jit(solution)/shard_map/ppermute | solution.py:20
  6.9 0.6 collective-permute-start
  7.6 9.6 %collective-permute-done = f32[8,2,1024]{2,1,0:T(2,128)S(1)} collective-permute-done((f32[8,2,1024]{2,1,0:T(2,128)S(1)}, f32[8,2,1024]{2,1,0:T(2,128)S(1)}, u32[]{:S(2)}, u32[]{:S(2)}) %collective-permute-start) | collective-permute-done | bytes 65568 | tf_op jit(solution)/shard_map/ppermute | solution.py:20
  17.4 3.7 %collective-permute-start.1 = (f32[10,2,1024]{2,1,0:T(2,128)S(1)}, f32[10,2,1024]{2,1,0:T(2,128)S(1)}, u32[]{:S(2)}, u32[]{:S(2)}) collective-permute-start(f32[10,2,1024]{2,1,0:T(2,128)S(1)} %pad_maximum_fusion.9), channel_id=1, source_target_pairs={{0,2},{1,3},{2,4},{3,5},{4,6},{5,7},{8,10},{9,11},{10,12},{11,13},... | collective-permute-start | bytes 245768 | tf_op jit(solution)/shard_map/ppermute | solution.py:15
  21.1 1.3 collective-permute-start.2
  22.5 0.6 collective-permute-done.1
  23.1 4.3 %collective-permute-done.2 = f32[10,2,1024]{2,1,0:T(2,128)S(1)} collective-permute-done((f32[10,2,1024]{2,1,0:T(2,128)S(1)}, f32[10,2,1024]{2,1,0:T(2,128)S(1)}, u32[]{:S(2)}, u32[]{:S(2)}) %collective-permute-start.2) | collective-permute-done | bytes 81952 | tf_op jit(solution)/shard_map/ppermute | solution.py:15
  29.0 0.4 broadcast_select_fusion.2
  29.4 1.6 collective-permute-start.3
  31.0 0.5 collective-permute-start.7
  31.6 3.5 %collective-permute-start.12 = (bf16[10,3,8,1024]{3,2,1,0:T(8,128)(2,1)S(1)}, bf16[10,3,8,1024]{3,2,1,0:T(8,128)(2,1)S(1)}, u32[]{:S(2)}, u32[]{:S(2)}) collective-permute-start(bf16[10,3,8,1024]{3,2,1,0:T(8,128)(2,1)S(1)} %pad_maximum_fusion.5), channel_id=1, source_target_pairs={{0,2},{1,3},{2,4},{3,5},{4,6},{5,7},{8,10},{9,11},{10,12},{11,13},... | collective-permute-start | bytes 1474568 | tf_op jit(solution)/shard_map/ppermute | solution.py:15
  35.2 1.3 collective-permute-start.13
  36.5 5.0 %collective-permute-done.3.other = bf16[8,3,8,1024]{3,2,1,0:T(8,128)(2,1)S(1)} collective-permute-done((bf16[8,3,8,1024]{3,2,1,0:T(8,128)(2,1)S(1)}, bf16[8,3,8,1024]{3,2,1,0:T(8,128)(2,1)S(1)}, u32[]{:S(2)}, u32[]{:S(2)}) %collective-permute-start.3) | collective-permute-done | bytes 393248 | tf_op jit(solution)/shard_map/ppermute | solution.py:20
  41.5 4.9 %collective-permute-done.7.other = bf16[8,3,8,1024]{3,2,1,0:T(8,128)(2,1)S(1)} collective-permute-done((bf16[8,3,8,1024]{3,2,1,0:T(8,128)(2,1)S(1)}, bf16[8,3,8,1024]{3,2,1,0:T(8,128)(2,1)S(1)}, u32[]{:S(2)}, u32[]{:S(2)}) %collective-permute-start.7) | collective-permute-done | bytes 393248 | tf_op jit(solution)/shard_map/ppermute | solution.py:20
  46.9 1.3 collective-permute-start.9
  48.3 1.3 collective-permute-start.5
  49.6 5.2 %collective-permute-start.4 = (bf16[10,3,8,1024]{3,2,1,0:T(8,128)(2,1)S(1)}, bf16[10,3,8,1024]{3,2,1,0:T(8,128)(2,1)S(1)}, u32[]{:S(2)}, u32[]{:S(2)}) collective-permute-start(bf16[10,3,8,1024]{3,2,1,0:T(8,128)(2,1)S(1)} %pad_maximum_fusion.1), channel_id=1, source_target_pairs={{0,2},{1,3},{2,4},{3,5},{4,6},{5,7},{8,10},{9,11},{10,12},{11,13},... | collective-permute-start | bytes 1474568 | tf_op jit(solution)/shard_map/ppermute | solution.py:15
  54.9 3.9 %collective-permute-start.8 = (bf16[10,3,8,1024]{3,2,1,0:T(8,128)(2,1)S(1)}, bf16[10,3,8,1024]{3,2,1,0:T(8,128)(2,1)S(1)}, u32[]{:S(2)}, u32[]{:S(2)}) collective-permute-start(bf16[10,3,8,1024]{3,2,1,0:T(8,128)(2,1)S(1)} %pad_maximum_fusion.3), channel_id=1, source_target_pairs={{0,2},{1,3},{2,4},{3,5},{4,6},{5,7},{8,10},{9,11},{10,12},{11,13},... | collective-permute-start | bytes 1474568 | tf_op jit(solution)/shard_map/ppermute | solution.py:15
  58.9 0.8 fusion
  59.6 0.6 pad_maximum_fusion.stat
  60.2 25.8 %smooth.5 = (bf16[8,3,8,1024]{3,2,1,0:T(8,128)(2,1)S(1)}, bf16[8,3,8,1024]{3,2,1,0:T(8,128)(2,1)S(1)}) custom-call(s32[2]{0:T(128)S(1)} %pad_add_fusion.2.info, f32[36,4,1024]{2,1,0:T(4,128)S(1)} %pad_maximum_fusion.stat, bf16[8,3,8,1024]{3,2,1,0:T(8,128)(2,1)S(1)} %get-tuple-element.15.keep, bf16[8,3,8,1024]{3,2,1,0:T(8,128)(2,1)S(1)} %collective-permute-done.11.other, ...), custom_call_target="tpu_custom_call" | custom-call | flops 61440000 | bytes 8388608 | tf_op jit(solution)/shard_map/smooth/pallas_call | solution.py:90
  86.2 1.6 collective-permute-start.14
  87.8 25.7 %smooth.3 = (bf16[8,3,8,1024]{3,2,1,0:T(8,128)(2,1)S(1)}, bf16[8,3,8,1024]{3,2,1,0:T(8,128)(2,1)S(1)}) custom-call(s32[2]{0:T(128)S(1)} %pad_add_fusion.info, f32[36,4,1024]{2,1,0:T(4,128)S(1)} %pad_maximum_fusion.stat, bf16[8,3,8,1024]{3,2,1,0:T(8,128)(2,1)S(1)} %get-tuple-element.23.keep, bf16[8,3,8,1024]{3,2,1,0:T(8,128)(2,1)S(1)} %collective-permute-done.3.other, ...), custom_call_target="tpu_custom_call" | custom-call | flops 61440000 | bytes 8388608 | tf_op jit(solution)/shard_map/smooth/pallas_call | solution.py:90
  113.8 25.8 %smooth.4 = (bf16[8,3,8,1024]{3,2,1,0:T(8,128)(2,1)S(1)}, bf16[8,3,8,1024]{3,2,1,0:T(8,128)(2,1)S(1)}) custom-call(s32[2]{0:T(128)S(1)} %pad_add_fusion.1.info, f32[36,4,1024]{2,1,0:T(4,128)S(1)} %pad_maximum_fusion.stat, bf16[8,3,8,1024]{3,2,1,0:T(8,128)(2,1)S(1)} %get-tuple-element.17.keep, bf16[8,3,8,1024]{3,2,1,0:T(8,128)(2,1)S(1)} %collective-permute-done.7.other, ...), custom_call_target="tpu_custom_call" | custom-call | flops 61440000 | bytes 8388608 | tf_op jit(solution)/shard_map/smooth/pallas_call | solution.py:90
  139.8 0.6 collective-permute-start.10
  140.6 1.6 collective-permute-start.6
  142.6 11.9 %collective-permute-done.6 = bf16[8,3,8,1024]{3,0,2,1:T(8,128)(2,1)S(1)} collective-permute-done((bf16[8,3,8,1024]{3,0,2,1:T(8,128)(2,1)S(1)}, bf16[8,3,8,1024]{3,0,2,1:T(8,128)(2,1)S(1)}, u32[]{:S(2)}, u32[]{:S(2)}) %collective-permute-start.6) | collective-permute-done | bytes 393248 | tf_op jit(solution)/shard_map/ppermute | solution.py:20
  155.1 1.0 slice-done.1
  156.1 6.5 %project.1 = f32[2,3,8,8,512]{4,3,2,1,0:T(8,128)S(1)} custom-call(bf16[3,45,8,1024]{3,2,1,0:T(8,128)(2,1)S(1)} %maximum_bitcast_fusion.fields, bf16[8,45,8,1024]{3,2,1,0:T(8,128)(2,1)S(1)} %bitcast.18), custom_call_target="tpu_custom_call" | custom-call | flops 17694720 | bytes 8110080 | tf_op jit(solution)/shard_map/project/pallas_call | solution.py:136
  162.8 1.7 %collective-permute-done.15 = f32[3,8,8,512]{3,2,1,0:T(8,128)S(1)} collective-permute-done((f32[3,8,8,512]{3,2,1,0:T(8,128)S(1)}, f32[3,8,8,512]{3,2,1,0:T(8,128)S(1)}, u32[]{:S(2)}, u32[]{:S(2)}) %collective-permute-start.15) | collective-permute-done | bytes 393248 | tf_op jit(solution)/shard_map/ppermute | solution.py:204
  164.6 0.8 pad_maximum_fusion.7
  (80 shorter events, 5.0 us)
Async XLA Ops:
  3.5 3.2 %copy-start.1 = (s32[8,1024]{1,0:T(8,128)S(1)}, s32[8,1024]{1,0:T(8,128)}, u32[]{:S(2)}) copy-start(s32[8,1024]{1,0:T(8,128)} %param.8) | copy-start | bytes 98308
  3.5 3.2 %copy-start.2 = (s32[8,1024]{1,0:T(8,128)S(1)}, s32[8,1024]{1,0:T(8,128)}, u32[]{:S(2)}) copy-start(s32[8,1024]{1,0:T(8,128)} %param.9) | copy-start | bytes 98308
  3.5 3.2 %copy-start.3 = (f32[8,1024]{1,0:T(8,128)S(1)}, f32[8,1024]{1,0:T(8,128)}, u32[]{:S(2)}) copy-start(f32[8,1024]{1,0:T(8,128)} %param.7) | copy-start | bytes 98308
  3.7 25.4 %collective-permute-start.11 = (bf16[8,3,8,1024]{3,2,1,0:T(8,128)(2,1)S(1)}, bf16[8,3,8,1024]{3,2,1,0:T(8,128)(2,1)S(1)}, u32[]{:S(2)}, u32[]{:S(2)}) collective-permute-start(bf16[8,3,8,1024]{3,2,1,0:T(8,128)(2,1)S(1)} %broadcast_select_fusion.3), channel_id=1, source_target_pairs={{0,1},{1,0},{2,3},{3,2},{4,5},{5,4},{6,7},{7,6},{8,9},{9,8},{10,11... | collective-permute-start | bytes 1179656 | tf_op jit(solution)/shard_map/ppermute | solution.py:20
  6.9 10.4 %collective-permute-start = (f32[8,2,1024]{2,1,0:T(2,128)S(1)}, f32[8,2,1024]{2,1,0:T(2,128)S(1)}, u32[]{:S(2)}, u32[]{:S(2)}) collective-permute-start(f32[8,2,1024]{2,1,0:T(2,128)S(1)} %pad_maximum_fusion.11), channel_id=1, source_target_pairs={{0,1},{1,0},{2,3},{3,2},{4,5},{5,4},{6,7},{7,6},{8,9},{9,8},{10,11... | collective-permute-start | bytes 196616 | tf_op jit(solution)/shard_map/ppermute | solution.py:20
  17.4 5.8 %collective-permute-start.1 = (f32[10,2,1024]{2,1,0:T(2,128)S(1)}, f32[10,2,1024]{2,1,0:T(2,128)S(1)}, u32[]{:S(2)}, u32[]{:S(2)}) collective-permute-start(f32[10,2,1024]{2,1,0:T(2,128)S(1)} %pad_maximum_fusion.9), channel_id=1, source_target_pairs={{0,2},{1,3},{2,4},{3,5},{4,6},{5,7},{8,10},{9,11},{10,12},{11,13},... | collective-permute-start | bytes 245768 | tf_op jit(solution)/shard_map/ppermute | solution.py:15
  21.1 6.3 %collective-permute-start.2 = (f32[10,2,1024]{2,1,0:T(2,128)S(1)}, f32[10,2,1024]{2,1,0:T(2,128)S(1)}, u32[]{:S(2)}, u32[]{:S(2)}) collective-permute-start(f32[10,2,1024]{2,1,0:T(2,128)S(1)} %pad_maximum_fusion.10), channel_id=1, source_target_pairs={{2,0},{3,1},{4,2},{5,3},{6,4},{7,5},{10,8},{11,9},{12,10},{13,11},... | collective-permute-start | bytes 245768 | tf_op jit(solution)/shard_map/ppermute | solution.py:15
  29.4 12.1 %collective-permute-start.3 = (bf16[8,3,8,1024]{3,2,1,0:T(8,128)(2,1)S(1)}, bf16[8,3,8,1024]{3,2,1,0:T(8,128)(2,1)S(1)}, u32[]{:S(2)}, u32[]{:S(2)}) collective-permute-start(bf16[8,3,8,1024]{3,2,1,0:T(8,128)(2,1)S(1)} %get-tuple-element.20), channel_id=1, source_target_pairs={{0,1},{1,0},{2,3},{3,2},{4,5},{5,4},{6,7},{7,6},{8,9},{9,8},{10,11... | collective-permute-start | bytes 1179656 | tf_op jit(solution)/shard_map/ppermute | solution.py:20
  31.0 15.5 %collective-permute-start.7 = (bf16[8,3,8,1024]{3,2,1,0:T(8,128)(2,1)S(1)}, bf16[8,3,8,1024]{3,2,1,0:T(8,128)(2,1)S(1)}, u32[]{:S(2)}, u32[]{:S(2)}) collective-permute-start(bf16[8,3,8,1024]{3,2,1,0:T(8,128)(2,1)S(1)} %get-tuple-element.21), channel_id=1, source_target_pairs={{0,1},{1,0},{2,3},{3,2},{4,5},{5,4},{6,7},{7,6},{8,9},{9,8},{10,11... | collective-permute-start | bytes 1179656 | tf_op jit(solution)/shard_map/ppermute | solution.py:20
  31.6 23.3 %collective-permute-start.12 = (bf16[10,3,8,1024]{3,2,1,0:T(8,128)(2,1)S(1)}, bf16[10,3,8,1024]{3,2,1,0:T(8,128)(2,1)S(1)}, u32[]{:S(2)}, u32[]{:S(2)}) collective-permute-start(bf16[10,3,8,1024]{3,2,1,0:T(8,128)(2,1)S(1)} %pad_maximum_fusion.5), channel_id=1, source_target_pairs={{0,2},{1,3},{2,4},{3,5},{4,6},{5,7},{8,10},{9,11},{10,12},{11,13},... | collective-permute-start | bytes 1474568 | tf_op jit(solution)/shard_map/ppermute | solution.py:15
  35.2 25.0 %collective-permute-start.13 = (bf16[10,3,8,1024]{3,2,1,0:T(8,128)(2,1)S(1)}, bf16[10,3,8,1024]{3,2,1,0:T(8,128)(2,1)S(1)}, u32[]{:S(2)}, u32[]{:S(2)}) collective-permute-start(bf16[10,3,8,1024]{3,2,1,0:T(8,128)(2,1)S(1)} %pad_maximum_fusion.6), channel_id=1, source_target_pairs={{2,0},{3,1},{4,2},{5,3},{6,4},{7,5},{10,8},{11,9},{12,10},{13,11},... | collective-permute-start | bytes 1474568 | tf_op jit(solution)/shard_map/ppermute | solution.py:15
  46.9 66.9 %collective-permute-start.9 = (bf16[10,3,8,1024]{3,2,1,0:T(8,128)(2,1)S(1)}, bf16[10,3,8,1024]{3,2,1,0:T(8,128)(2,1)S(1)}, u32[]{:S(2)}, u32[]{:S(2)}) collective-permute-start(bf16[10,3,8,1024]{3,2,1,0:T(8,128)(2,1)S(1)} %pad_maximum_fusion.4), channel_id=1, source_target_pairs={{2,0},{3,1},{4,2},{5,3},{6,4},{7,5},{10,8},{11,9},{12,10},{13,11},... | collective-permute-start | bytes 1474568 | tf_op jit(solution)/shard_map/ppermute | solution.py:15
  48.3 39.5 %collective-permute-start.5 = (bf16[10,3,8,1024]{3,2,1,0:T(8,128)(2,1)S(1)}, bf16[10,3,8,1024]{3,2,1,0:T(8,128)(2,1)S(1)}, u32[]{:S(2)}, u32[]{:S(2)}) collective-permute-start(bf16[10,3,8,1024]{3,2,1,0:T(8,128)(2,1)S(1)} %pad_maximum_fusion.2), channel_id=1, source_target_pairs={{2,0},{3,1},{4,2},{5,3},{6,4},{7,5},{10,8},{11,9},{12,10},{13,11},... | collective-permute-start | bytes 1474568 | tf_op jit(solution)/shard_map/ppermute | solution.py:15
  49.6 38.1 %collective-permute-start.4 = (bf16[10,3,8,1024]{3,2,1,0:T(8,128)(2,1)S(1)}, bf16[10,3,8,1024]{3,2,1,0:T(8,128)(2,1)S(1)}, u32[]{:S(2)}, u32[]{:S(2)}) collective-permute-start(bf16[10,3,8,1024]{3,2,1,0:T(8,128)(2,1)S(1)} %pad_maximum_fusion.1), channel_id=1, source_target_pairs={{0,2},{1,3},{2,4},{3,5},{4,6},{5,7},{8,10},{9,11},{10,12},{11,13},... | collective-permute-start | bytes 1474568 | tf_op jit(solution)/shard_map/ppermute | solution.py:15
  54.9 58.9 %collective-permute-start.8 = (bf16[10,3,8,1024]{3,2,1,0:T(8,128)(2,1)S(1)}, bf16[10,3,8,1024]{3,2,1,0:T(8,128)(2,1)S(1)}, u32[]{:S(2)}, u32[]{:S(2)}) collective-permute-start(bf16[10,3,8,1024]{3,2,1,0:T(8,128)(2,1)S(1)} %pad_maximum_fusion.3), channel_id=1, source_target_pairs={{0,2},{1,3},{2,4},{3,5},{4,6},{5,7},{8,10},{9,11},{10,12},{11,13},... | collective-permute-start | bytes 1474568 | tf_op jit(solution)/shard_map/ppermute | solution.py:15
  86.2 68.4 %collective-permute-start.14 = (bf16[8,3,8,1024]{3,0,2,1:T(8,128)(2,1)S(1)}, bf16[8,3,8,1024]{3,0,2,1:T(8,128)(2,1)S(1)}, u32[]{:S(2)}, u32[]{:S(2)}) collective-permute-start(bf16[8,3,8,1024]{3,0,2,1:T(8,128)(2,1)S(1)} %copy.27), channel_id=1, source_target_pairs={{0,1},{1,0},{2,3},{3,2},{4,5},{5,4},{6,7},{7,6},{8,9},{9,8},{10,11... | collective-permute-start | bytes 1179656 | tf_op jit(solution)/shard_map/ppermute | solution.py:20
  139.8 14.8 %collective-permute-start.10 = (bf16[8,3,8,1024]{3,0,2,1:T(8,128)(2,1)S(1)}, bf16[8,3,8,1024]{3,0,2,1:T(8,128)(2,1)S(1)}, u32[]{:S(2)}, u32[]{:S(2)}) collective-permute-start(bf16[8,3,8,1024]{3,0,2,1:T(8,128)(2,1)S(1)} %copy.26), channel_id=1, source_target_pairs={{0,1},{1,0},{2,3},{3,2},{4,5},{5,4},{6,7},{7,6},{8,9},{9,8},{10,11... | collective-permute-start | bytes 1179656 | tf_op jit(solution)/shard_map/ppermute | solution.py:20
  140.4 14.8 %slice-start = ((s8[5898240]{0:T(1024)(128)(4,1)}), s8[4194304]{0:T(1024)(128)(4,1)S(1)}, s32[]{:S(2)}) async-start(s8[5898240]{0:T(1024)(128)(4,1)} %bitcast.17), calls=%async_computation | async-start | bytes 8388608
  140.6 13.9 %collective-permute-start.6 = (bf16[8,3,8,1024]{3,0,2,1:T(8,128)(2,1)S(1)}, bf16[8,3,8,1024]{3,0,2,1:T(8,128)(2,1)S(1)}, u32[]{:S(2)}, u32[]{:S(2)}) collective-permute-start(bf16[8,3,8,1024]{3,0,2,1:T(8,128)(2,1)S(1)} %copy.25), channel_id=1, source_target_pairs={{0,1},{1,0},{2,3},{3,2},{4,5},{5,4},{6,7},{7,6},{8,9},{9,8},{10,11... | collective-permute-start | bytes 1179656 | tf_op jit(solution)/shard_map/ppermute | solution.py:20
  154.6 1.5 slice-start.1
  156.1 6.5 %copy-start = (bf16[3,45,8,1024]{3,2,1,0:T(8,128)(2,1)}, bf16[3,45,8,1024]{3,2,1,0:T(8,128)(2,1)S(1)}, u32[]{:S(2)}) copy-start(bf16[3,45,8,1024]{3,2,1,0:T(8,128)(2,1)S(1)} %maximum_bitcast_fusion.fields) | copy-start | bytes 6635524
  162.7 1.8 %collective-permute-start.15 = (f32[3,8,8,512]{3,2,1,0:T(8,128)S(1)}, f32[3,8,8,512]{3,2,1,0:T(8,128)S(1)}, u32[]{:S(2)}, u32[]{:S(2)}) collective-permute-start(f32[3,8,8,512]{3,2,1,0:T(8,128)S(1)} %dynamic-slice_bitcast_fusion), channel_id=1, source_target_pairs={{0,8},{8,0},{1,9},{9,1},{2,10},{10,2},{3,11},{11,3},{4,12},{12,4},... | collective-permute-start | bytes 1179656 | tf_op jit(solution)/shard_map/ppermute | solution.py:204
